TPU v7x, 32 devices: a whole 2x2x4 slice. The times are simulated.
32 devices in a mesh: cent: 4 (over y, x), rows: 8 (over z, core).
Axes of the slice: x: 2, y: 2, z: 4, core: 2. Of those that a mesh axis runs over, the one named last changes fastest.
Arguments:
- embeddings: bfloat16 [8192, 2048], P(('cent', 'rows')), may hold values from -6 to 6
- centroids: bfloat16 [4096, 2048], P(('cent', 'rows')), may hold values from -0.125 to 0.125
- cluster: int32 [8192, 1], P(('cent', 'rows')), may hold values from 0 to 31; in each aligned block of 256 rows (0 to 255, 256 to 511, ...) at most 16 rows name the same one
- noise_salt: int32 [1], replicated, may hold values from 0 to 1048575
Outputs:
- perturbed_max: float32 [8192], P(('cent', 'rows'))
- dedup_score: float32 [8192], P(('cent', 'rows'))
- new_centroids: float32 [32, 2048], P(('cent', 'rows'))
Inputs may be any that keep to these rules, and one draw needn't show every extreme that they name: In every aligned block of 256 rows (the rows of one device) no cluster is named by more than 16 rows, and in some block some cluster by exactly 16; every cluster is named by some row.
All inputs are finite; a program needn't handle non-finite values.
Results may differ from a plain program's by a relative error of at most 0.0003.
Values may be sent and summed in bfloat16 or wider, within the bound.
No kernel may reach another device: no remote copies, remote signals or barrier semaphores. Data moves between devices by JAX's collectives and lax.ppermute only.
A program may use at most 128 MiB of HBM per device.

v0:
```python
import math

import jax
import jax.numpy as jnp
from jax import lax
from jax.sharding import PartitionSpec as P

inverse_temp = 3.0
epsilon = 1e-06


def logical_shift(word, amount):
    return lax.shift_right_logical(word, jnp.full(word.shape, amount, jnp.int32))


def gumbel_noise(row_ids, cent_ids, salt_word):
    mixed = row_ids * 1103515245 + cent_ids * 739982445 + salt_word
    mixed = mixed ^ logical_shift(mixed, 16)
    mixed = mixed * 2146121005
    mixed = mixed ^ logical_shift(mixed, 15)
    mixed = mixed * 1759714725
    mixed = mixed ^ logical_shift(mixed, 16)
    low_bits = mixed & 8388607
    uniform = (low_bits.astype(jnp.float32) + 0.5) * (1.0 / 8388608.0)
    return -jnp.log(-jnp.log(uniform))


def cluster_stats(members, valid):
    feature_dim = members.shape[1]
    widened = members.astype(jnp.float32)
    scale = lax.rsqrt(jnp.mean(widened * widened, axis=1) + epsilon)
    gram = lax.dot_general(
        members, members, (((1,), (1,)), ((), ())), preferred_element_type=jnp.float32
    )
    similar = gram * scale[:, None] * scale[None, :] * (1.0 / math.sqrt(feature_dim))
    order = jnp.arange(members.shape[0], dtype=jnp.int32)
    usable = valid[None, :] & (order[:, None] != order[None, :])
    highest = jnp.max(jnp.where(usable, similar, -1e30), axis=1)
    scores = jnp.where(jnp.any(usable, axis=1), highest, 0.0)
    total = jnp.sum(jnp.where(valid[:, None], widened, 0.0), axis=0)
    center = total * lax.rsqrt(jnp.mean(total * total) + epsilon)
    return (scores, center)


def shards(embeddings, centroids, cluster, noise_salt):
    rows_dev, feature_dim = embeddings.shape
    cent_dev = centroids.shape[0]
    cent_count = lax.axis_size("cent")
    rows_count = lax.axis_size("rows")
    devices = cent_count * rows_count
    capacity = max(2, 2 * rows_dev // devices)
    cent_index = lax.axis_index("cent")
    rows_index = lax.axis_index("rows")
    salt_word = noise_salt[0]
    group = lax.all_gather(embeddings, "cent", axis=0, tiled=True)
    position = jnp.arange(cent_count * rows_dev, dtype=jnp.int32)
    group_ids = (position // rows_dev * rows_count + rows_index) * rows_dev + position % rows_dev
    panel_base = cent_index * (rows_count * cent_dev)
    initial = jnp.full((cent_count * rows_dev,), -1e30, jnp.float32)
    piece = lax.all_gather(centroids, "rows", axis=0, tiled=True)
    piece_rows = piece.shape[0]
    block = math.gcd(piece_rows, 512)
    tiles = piece.reshape(piece_rows // block, block, feature_dim)
    offsets = jnp.arange(piece_rows // block, dtype=jnp.int32) * block

    def step(carry, item):
        tile, offset = item
        scores = lax.dot_general(
            group, tile, (((1,), (1,)), ((), ())), preferred_element_type=jnp.float32
        )
        cent_ids = panel_base + offset + jnp.arange(block, dtype=jnp.int32)
        perturbed = inverse_temp * scores + gumbel_noise(
            group_ids[:, None], cent_ids[None, :], salt_word
        )
        return (jnp.maximum(carry, jnp.max(perturbed, axis=1)), None)

    result, unused = lax.scan(step, initial, (tiles, offsets))
    merged = lax.pmax(result, "cent")
    perturbed_max = lax.dynamic_slice_in_dim(merged, cent_index * rows_dev, rows_dev)
    assigned = cluster[:, 0]
    order = jnp.arange(rows_dev, dtype=jnp.int32)
    same = (assigned[:, None] == assigned[None, :]) & (order[None, :] < order[:, None])
    rank = jnp.sum(same.astype(jnp.int32), axis=1)
    slot = assigned * capacity + rank
    outgoing = jnp.zeros((devices * capacity, feature_dim), jnp.bfloat16).at[slot].set(embeddings)
    present = (
        jnp.zeros((devices * capacity,), jnp.bfloat16)
        .at[slot]
        .set(jnp.ones((rows_dev,), jnp.bfloat16))
    )
    received, arrived = (
        lax.all_to_all(
            outgoing.reshape(devices, capacity, feature_dim),
            ("cent", "rows"),
            split_axis=0,
            concat_axis=0,
            tiled=True,
        ),
        lax.all_to_all(
            present.reshape(devices, capacity),
            ("cent", "rows"),
            split_axis=0,
            concat_axis=0,
            tiled=True,
        ),
    )
    members = received.reshape(devices * capacity, feature_dim)
    valid = arrived.reshape(devices * capacity) > 0.5
    scores, center = cluster_stats(members, valid)
    returned = lax.all_to_all(
        scores.reshape(devices, capacity), ("cent", "rows"), split_axis=0, concat_axis=0, tiled=True
    )
    dedup_score = returned.reshape(devices * capacity)[slot]
    return (perturbed_max, dedup_score, center[None, :])


def solution(mesh):
    in_specs = (
        P(("cent", "rows"), None),
        P(("cent", "rows"), None),
        P(("cent", "rows"), None),
        P(),
    )
    out_specs = (P(("cent", "rows")), P(("cent", "rows")), P(("cent", "rows"), None))
    return jax.shard_map(shards, mesh=mesh, in_specs=in_specs, out_specs=out_specs, check_vma=False)
```

profile of v0, /device:TPU:0, one launch (start us, length us, event | category | flops | bytes accessed | tf_op | source)
XLA Modules:
  0.0 164.9 jit_solution(17249637554160491330)
XLA Ops:
  7.2 0.7 all-gather.5.cloned.1.call-update
  7.9 0.7 all-gather.3.cloned.1.call-update
  8.6 0.9 convert_reduce_fusion
  9.6 0.7 compare_select_fusion
  10.3 2.2 %scatter_custom_fusion = bf16[512]{0:T(512)(128)(2,1)S(1)} fusion(s32[256]{0:T(256)S(1)} %bitcast.38, bf16[256]{0:T(256)(128)(2,1)S(1)} %broadcast.128, bf16[]{:T(256)} %constant.95.clone.1), kind=kCustom, calls=%fused_computation.65 | custom fusion | bytes 1026 | tf_op jit(solution)/shard_map/scatter | solution.py:89
  12.4 0.7 all_to_all.17
  13.1 7.3 %all-to-all-start = ((bf16[32,1,16]{2,1,0:T(2,128)(2,1)}), bf16[32,1,16]{2,1,0:T(2,128)(2,1)S(1)}, u32[]{:S(2)}, u32[]{:S(2)}) async-start(bf16[32,1,16]{2,1,0:T(2,128)(2,1)} %all_to_all.17), calls=%async_computation | async-start | bytes 32768 | tf_op jit(solution)/shard_map/all_to_all | solution.py:99
  20.4 4.5 %scatter_custom_fusion.1 = bf16[512,2048]{1,0:T(8,128)(2,1)} fusion(s32[256]{0:T(256)S(1)} %bitcast.39, bf16[256,2048]{1,0:T(8,128)(2,1)} %param.6, bf16[]{:T(256)} %constant.95.clone.1), kind=kCustom, calls=%fused_computation.50 | custom fusion | bytes 2097664 | tf_op jit(solution)/shard_map/scatter | solution.py:85
  24.9 2.6 %all-to-all-done = bf16[32,1,16]{2,1,0:T(2,128)(2,1)S(1)} async-done(((bf16[32,1,16]{2,1,0:T(2,128)(2,1)}), bf16[32,1,16]{2,1,0:T(2,128)(2,1)S(1)}, u32[]{:S(2)}, u32[]{:S(2)}) %all-to-all-start) | async-done | bytes 1056 | tf_op jit(solution)/shard_map/all_to_all | solution.py:99
  27.6 3.2 %all-to-all-start.1 = ((bf16[32,16,2048]{2,1,0:T(8,128)(2,1)}), bf16[32,16,2048]{2,1,0:T(8,128)(2,1)S(1)}, u32[]{:S(2)}, u32[]{:S(2)}) async-start(bf16[32,16,2048]{2,1,0:T(8,128)(2,1)} %bitcast.35), calls=%async_computation.1 | async-start | bytes 4194304 | tf_op jit(solution)/shard_map/all_to_all | solution.py:92
  30.9 0.1 copy.16
  31.0 0.1 gt.22
  31.2 0.2 fusion.41
  31.4 49.7 %all-to-all-done.1 = bf16[32,16,2048]{2,1,0:T(8,128)(2,1)S(1)} async-done(((bf16[32,16,2048]{2,1,0:T(8,128)(2,1)}), bf16[32,16,2048]{2,1,0:T(8,128)(2,1)S(1)}, u32[]{:S(2)}, u32[]{:S(2)}) %all-to-all-start.1) | async-done | bytes 2097184 | tf_op jit(solution)/shard_map/all_to_all | solution.py:92
  81.0 0.8 fusion.33
  82.0 1.4 fusion.37
  83.4 0.7 select_n.51
  84.0 2.5 %all-to-all-start.2 = ((f32[32,1,16]{2,1,0:T(1,128)}), f32[32,1,16]{2,1,0:T(1,128)S(1)}, u32[]{:S(2)}, u32[]{:S(2)}) async-start(f32[32,1,16]{2,1,0:T(1,128)} %bitcast.7), calls=%async_computation.2 | async-start | bytes 32768 | tf_op jit(solution)/shard_map/all_to_all | solution.py:110
  86.5 0.6 multiply_reduce_fusion
  87.8 0.6 broadcast_multiply_fusion
  88.4 5.2 %all-to-all-done.2 = f32[32,1,16]{2,1,0:T(1,128)S(1)} async-done(((f32[32,1,16]{2,1,0:T(1,128)}), f32[32,1,16]{2,1,0:T(1,128)S(1)}, u32[]{:S(2)}, u32[]{:S(2)}) %all-to-all-start.2) | async-done | bytes 2080 | tf_op jit(solution)/shard_map/all_to_all | solution.py:110
  93.7 0.5 broadcast.165
  94.2 0.7 reduce.5
  94.9 2.5 %gather_fusion = f32[256]{0:T(256)} fusion(f32[512]{0:T(512)S(1)} %reshape.115, s32[1024]{0:T(1024)S(1)} %pad_clamp_fusion), kind=kCustom, calls=%fused_computation | custom fusion | bytes 3072 | tf_op jit(solution)/shard_map/gather | solution.py:113
  97.5 33.7 %all-gather.3.cloned.1.call-done = bf16[1024,2048]{1,0:T(8,128)(2,1)} async-done(((bf16[128,2048]{1,0:T(8,128)(2,1)}), bf16[1024,2048]{1,0:T(8,128)(2,1)}) %all-gather.3.cloned.1.call-update) | async-done | bytes 4194320 | tf_op jit(solution)/shard_map/all_gather | solution.py:60
  131.1 16.2 %while.11 = (s32[]{:T(128)}, f32[1024]{0:T(1024)S(1)}, bf16[2,512,2048]{2,1,0:T(8,128)(2,1)}, bf16[1024,2048]{1,0:T(8,128)(2,1)}, s32[2]{0:T(128)S(1)}, /*index=...) while((s32[]{:T(128)}, f32[1024]{0:T(1024)S(1)}, bf16[2,512,2048]{2,1,0:T(8,128)(2,1)}, ...), condition=%wide.region_2.3_spmd.clone, body=%wide.region_0.2_spmd.clone.sunk | while | flops 2157464576 | bytes 6320795 | solution.py:77
  131.1 0.6 dynamic_slice.23
  132.3 6.9 %fusion.56 = f32[1024]{0:T(1024)S(1)} fusion(bf16[1024,2048]{1,0:T(8,128)(2,1)} %get-tuple-element.166, bf16[2,512,2048]{2,1,0:T(8,128)(2,1)} %get-tuple-element.165, s32[]{:T(128)S(6)} %copy.21, s32[]{:T(128)} %get-tuple-element.169, s32[512]{0:T(512)S(1)} %add_multiply_fusion.2, s32[1024]{0:T(1024)S(1)} %fusion.55), kind=kOutput, calls=%fused_computation.21.clone.1 | convolution fusion | flops 2157444096 | bytes 6302212 | tf_op jit(solution)/shard_map/while/body/eval_jaxpr/dot_general | solution.py:68
  139.2 0.6 dynamic_slice.23
  140.4 6.9 %fusion.56 = f32[1024]{0:T(1024)S(1)} fusion(bf16[1024,2048]{1,0:T(8,128)(2,1)} %get-tuple-element.166, bf16[2,512,2048]{2,1,0:T(8,128)(2,1)} %get-tuple-element.165, s32[]{:T(128)S(6)} %copy.21, s32[]{:T(128)} %get-tuple-element.169, s32[512]{0:T(512)S(1)} %add_multiply_fusion.2, s32[1024]{0:T(1024)S(1)} %fusion.55), kind=kOutput, calls=%fused_computation.21.clone.1 | convolution fusion | flops 2157444096 | bytes 6302212 | tf_op jit(solution)/shard_map/while/body/eval_jaxpr/dot_general | solution.py:68
  147.4 10.1 %pmax.7 = f32[1024]{0:T(1024)S(1)} all-reduce(f32[1024]{0:T(1024)S(1)} %get-tuple-element.45), channel_id=1, replica_groups=mesh['cent'=4,'rows'=8] {'cent'}, use_global_device_ids=true, to_apply=%region_3.4 | all-reduce | flops 1024 | bytes 8192 | tf_op jit(solution)/shard_map/pmax | solution.py:78
  157.4 0.6 dynamic_slice.11
  (21 shorter events, 0.5 us)
Async XLA Ops:
  7.2 90.3 %all-gather.5.cloned.1.call-start = ((), (), s32[]{:S(2)}) async-start(), calls=%async_computation.4 | async-start | bytes 5242880 | tf_op jit(solution)/shard_map/all_gather | solution.py:55
  7.9 123.2 %all-gather.3.cloned.1.call-start = ((), (), s32[]{:S(2)}) async-start(), calls=%async_computation.3 | async-start | bytes 4718592 | tf_op jit(solution)/shard_map/all_gather | solution.py:60
  13.1 14.4 %all-to-all-start = ((bf16[32,1,16]{2,1,0:T(2,128)(2,1)}), bf16[32,1,16]{2,1,0:T(2,128)(2,1)S(1)}, u32[]{:S(2)}, u32[]{:S(2)}) async-start(bf16[32,1,16]{2,1,0:T(2,128)(2,1)} %all_to_all.17), calls=%async_computation | async-start | bytes 32768 | tf_op jit(solution)/shard_map/all_to_all | solution.py:99
  27.6 53.4 %all-to-all-start.1 = ((bf16[32,16,2048]{2,1,0:T(8,128)(2,1)}), bf16[32,16,2048]{2,1,0:T(8,128)(2,1)S(1)}, u32[]{:S(2)}, u32[]{:S(2)}) async-start(bf16[32,16,2048]{2,1,0:T(8,128)(2,1)} %bitcast.35), calls=%async_computation.1 | async-start | bytes 4194304 | tf_op jit(solution)/shard_map/all_to_all | solution.py:92
  84.0 9.6 %all-to-all-start.2 = ((f32[32,1,16]{2,1,0:T(1,128)}), f32[32,1,16]{2,1,0:T(1,128)S(1)}, u32[]{:S(2)}, u32[]{:S(2)}) async-start(f32[32,1,16]{2,1,0:T(1,128)} %bitcast.7), calls=%async_computation.2 | async-start | bytes 32768 | tf_op jit(solution)/shard_map/all_to_all | solution.py:110
Sparse Core Ops, SparseCore 0:
  9.8 72.6 all-gather.4
  84.1 46.9 all-gather.2
where the time goes:
time: 165 us
  waiting for transfers between devices  92.6 us (56%)
  matrix products  15.3 us (9%)
  between operations  14.8 us (9%)
  local copies, waits for them, and re-layouts  13.3 us (8%)
  starting transfers between devices  13 us (8%)
  blocking collectives  10.1 us (6%)
  other arithmetic  4.58 us (3%)
    all_to_all x1, waiting for transfers between devices, shards(): lax.all_to_all(outgoing.reshape(devices, capacity, feature_dim), ('cent',...  49.7 us
    all_gather x1, waiting for transfers between devices, shards(): piece = lax.all_gather(centroids, 'rows', axis=0, tiled=True)  33.7 us
    dot_general x2, matrix products, step(): lax.dot_general(group, tile, (((1,), (1,)), ((), ())), preferred_element_...  13.9 us
    pmax x1, blocking collectives, shards(): merged = lax.pmax(result, 'cent')  10.1 us
    all_to_all x1, starting transfers between devices, shards(): lax.all_to_all(present.reshape(devices, capacity), ('cent', 'rows'), spli...  7.3 us
    all_to_all x1, waiting for transfers between devices, shards(): lax.all_to_all(scores.reshape(devices, capacity), ('cent', 'rows'), split...  5.25 us
    scatter x1, local copies, waits for them, and re-layouts, shards(): jnp.zeros((devices * capacity, feature_dim), jnp.bfloat16).at[slot]  4.51 us
  transfers between devices with their start and end apart: 5, of which 4 were waited for; matrix products, arithmetic and copies ran while one was open for 10% of the time, Pallas kernels for 0%

commit v1 on v0

--- a/solution.py
+++ b/solution.py
@@ -3,6 +3,8 @@
 import jax
 import jax.numpy as jnp
 from jax import lax
+from jax.experimental import pallas as pl
+from jax.experimental.pallas import tpu as pltpu
 from jax.sharding import PartitionSpec as P
 
 inverse_temp = 3.0
@@ -114,12 +116,351 @@
     return (perturbed_max, dedup_score, center[None, :])
 
 
+lowest = -1e30
+VMEM = pl.BlockSpec(memory_space=pltpu.VMEM)
+SMEM = pl.BlockSpec(memory_space=pltpu.SMEM)
+
+
+def product(left, right):
+    return lax.dot_general(left, right, (((1,), (1,)), ((), ())), preferred_element_type=jnp.float32)
+
+
+def top(values):
+    return jnp.max(values, axis=0, keepdims=True)
+
+
+def read_note(note):
+    words = note[:, 0:1024].astype(jnp.float32)
+    scale = words[:, 256:512] + words[:, 512:768] + words[:, 768:1024]
+    return words[:, 0:256], scale
+
+
+def as_columns(note):
+    cluster, scale = read_note(note)
+    return cluster.T[:, 0:1], scale.T[:, 0:1]
+
+
+def note_kernel(emb, cluster, own_out, scale_out):
+    rows = emb.shape[0]
+    total = jnp.zeros((rows, 128), jnp.float32)
+    for at in range(0, emb.shape[1], 128):
+        piece = emb[:, at : at + 128]
+        own_out[pl.ds(0, rows), at : at + 128] = piece
+        piece = piece.astype(jnp.float32)
+        total = total + piece * piece
+    mean = jnp.sum(total.T, axis=0, keepdims=True) * (1.0 / emb.shape[1])
+    scale = lax.rsqrt(mean + epsilon)
+    scale_out[...] = scale
+    high = scale.astype(jnp.bfloat16)
+    rest = scale - high.astype(jnp.float32)
+    middle = rest.astype(jnp.bfloat16)
+    low = (rest - middle.astype(jnp.float32)).astype(jnp.bfloat16)
+    named = cluster[...].astype(jnp.float32).astype(jnp.bfloat16)
+    zeros = jnp.zeros((8, 1024), jnp.bfloat16)
+    line = jnp.concatenate([named, high, middle, low], axis=1)
+    own_out[pl.ds(rows, 8), :] = jnp.concatenate([jnp.broadcast_to(line, (8, 1024)), zeros], axis=1)
+
+
+def blocks_of(whole, split):
+    pieces = [(ref, 0, 256) for ref in whole]
+    notes = [ref[pl.ds(256, 8), :] for ref in whole]
+    for first, second in split:
+        pieces += [(first, 128, 128), (second, 128, 128)]
+        notes.append(second[pl.ds(256, 8), :])
+    return pieces, notes
+
+
+def stack(pieces):
+    return jnp.concatenate([ref[pl.ds(lo, rows), :] for ref, lo, rows in pieces], axis=0)
+
+
+def write_columns(columns, notes):
+    for index, note in enumerate(notes):
+        rows = pl.ds(256 * index, 256)
+        for lo, value in zip((0, 128), as_columns(note)):
+            columns[rows, lo : lo + 128] = jnp.broadcast_to(value, (256, 128))
+
+
+def read_columns(columns):
+    return tuple(jnp.concatenate([columns[:, lo : lo + 128]] * 2, axis=1) for lo in (0, 128))
+
+
+def similarity(pieces, columns, rows, cluster, same=False):
+    grams = product(stack(pieces), rows)
+    of_cluster, scale = read_columns(columns)
+    usable = of_cluster == cluster
+    if same:
+        shape = grams.shape
+        usable = usable & (lax.broadcasted_iota(jnp.int32, shape, 0) != lax.broadcasted_iota(jnp.int32, shape, 1))
+    return top(jnp.where(usable, grams * scale, lowest))
+
+
+def sums_of(pos, pieces, notes):
+    named = jnp.concatenate([read_note(note)[0][0:1] for note in notes], axis=1)
+    owned = pos[0] * 8 + 2 * lax.broadcasted_iota(jnp.int32, (8, named.shape[1]), 0) + pos[1] % 2
+    chosen = (owned.astype(jnp.float32) == named).astype(jnp.bfloat16)
+    return jnp.dot(chosen, stack(pieces), preferred_element_type=jnp.float32)
+
+
+def named_rows(ref):
+    return ref[pl.ds(0, 256), :], read_note(ref[pl.ds(256, 8), :])[0][0:1]
+
+
+def choose(target, first, second, pos):
+    layer = pos[1] // 2
+    mid = (layer == 1) | (layer == 2)
+
+    @pl.when(mid)
+    def _():
+        target[...] = first[...]
+
+    @pl.when(jnp.logical_not(mid))
+    def _():
+        target[...] = second[...]
+
+    return mid
+
+
+def in_the_middle(pos):
+    layer = pos[1] // 2
+    return (layer == 1) | (layer == 2)
+
+
+def early_kernel(pos, own, own_s, gx, gx_s, x0, m1, sims, sums, columns):
+    pieces, notes = blocks_of((own, own_s, gx, gx_s), ())
+    write_columns(columns, notes)
+    for number, ref in enumerate((own, x0)):
+        sims[number] = similarity(pieces, columns, *named_rows(ref), same=number == 0)
+    sims[2] = jnp.full((1, 256), lowest, jnp.float32)
+
+    @pl.when(in_the_middle(pos))
+    def _():
+        sims[2] = similarity(pieces, columns, *named_rows(m1))
+
+    sums[...] = sums_of(pos, pieces, notes)
+
+
+def first_kernel(
+    pos, own, own_s, gx, gx_s, gy, gy_s, hx, hx_s, hy, hy_s, cents, cents_s, x0, m1, x1, m3, noise, noise_far, early,
+    early_sums, early_columns, result, sums, columns, near,
+):
+    mid = choose(near, m1, x1, pos)
+    pieces, notes = blocks_of((gy, gy_s), ((hy, hx), (hy_s, hx_s)))
+    write_columns(columns, notes)
+    before = blocks_of((own, own_s, gx, gx_s), ())[0]
+    cent_pieces = [(ref, 0, 128) for ref in (cents, cents_s, hx, hx_s, hy, hy_s)]
+    for number, ref in enumerate((own, x0, near)):
+        rows, cluster = named_rows(ref)
+        sim = similarity(pieces, columns, rows, cluster)
+        lanes = slice(256 * number, 256 * number + 256)
+        score = top(inverse_temp * product(stack(cent_pieces), rows) + noise[:, lanes])
+        result[number] = jnp.concatenate([score, jnp.maximum(sim, early[number])], axis=0)
+    sums[...] = early_sums[...] + sums_of(pos, pieces, notes)
+
+    @pl.when(mid)
+    def _():
+        rows, cluster = named_rows(m3)
+        sim = jnp.maximum(similarity(before, early_columns, rows, cluster), similarity(pieces, columns, rows, cluster))
+        score = top(inverse_temp * product(stack(cent_pieces), rows) + noise_far[0:768, :])
+        result[3] = jnp.concatenate([score, sim], axis=0)
+
+    @pl.when(jnp.logical_not(mid))
+    def _():
+        sim = similarity(before, early_columns, *named_rows(near))
+        result[2] = jnp.concatenate([result[2][0:1], jnp.maximum(result[2][1:2], sim)], axis=0)
+
+
+def whole_visit(rows, cluster, layer_refs, columns, noise):
+    own, own_s, gx, gx_s, gy, gy_s, hx, hx_s, hy, hy_s, cents, cents_s, d, d_s = layer_refs
+    first = blocks_of((own, own_s, gx, gx_s), ())[0]
+    second = blocks_of((gy, gy_s), ((hy, hx), (hy_s, hx_s)))[0]
+    sim = similarity(first, columns[0], rows, cluster)
+    sim = jnp.maximum(sim, similarity(second, columns[1], rows, cluster))
+    pieces = [(ref, 0, 128) for ref in (cents, cents_s, hx, hx_s, hy, hy_s, d, d_s)]
+    return top(inverse_temp * product(stack(pieces), rows) + noise[...]), sim
+
+
+def second_kernel(
+    pos, own, x0, m1, x1, m3, d, d_s, noise, noise_far, before, sums, mine, by_one, by_two, by_three, near,
+):
+    mid = choose(near, m1, x1, pos)
+    layer = pos[1] // 2
+    cents = stack([(d, 0, 128), (d_s, 0, 128)])
+
+    def visit(number, ref, values):
+        score = top(inverse_temp * product(cents, ref[pl.ds(0, 256), :]) + values)
+        return jnp.maximum(score, before[number][0:1]), before[number][1:2]
+
+    results = [visit(i, ref, noise[:, 256 * i : 256 * i + 256]) for i, ref in enumerate((own, x0, near))]
+    mine[:, 0:256], mine[:, 256:512] = results[0]
+    by_one[:, 0:256], by_one[:, 256:512] = results[1]
+    for bits, out in ((0, mine), (1, by_one), (2, by_two), (3, by_three)):
+        out[:, 512:] = sums[pl.ds(layer ^ bits, 1), :]
+
+    @pl.when(mid)
+    def _():
+        by_three[:, 0:256], by_three[:, 256:512] = results[2]
+        by_two[:, 0:256], by_two[:, 256:512] = visit(3, m3, noise_far[768:1024, :])
+
+    @pl.when(jnp.logical_not(mid))
+    def _():
+        by_two[:, 0:256], by_two[:, 256:512] = results[2]
+        by_three[:, 0:512] = jnp.full((1, 512), lowest, jnp.float32)
+
+
+def last_kernel(*refs):
+    pos, layer_refs, (x2, noise_far), columns, (before, out) = refs[0], refs[1:15], refs[15:17], refs[17:19], refs[19:]
+    layer = pos[1] // 2
+    out[...] = before[...]
+
+    @pl.when((layer == 0) | (layer == 3))
+    def _():
+        rows, cluster = named_rows(x2)
+        out[:, 0:256], out[:, 256:512] = whole_visit(rows, cluster, layer_refs, columns, noise_far)
+
+
+def final_kernel(scale, *refs):
+    parts, (score_out, sim_out, center_out) = refs[:4], refs[4:]
+    score, sim, total = parts[0][:, 0:256], parts[0][:, 256:512], parts[0][:, 512:]
+    for part in parts[1:]:
+        score = jnp.maximum(score, part[:, 0:256])
+        sim = jnp.maximum(sim, part[:, 256:512])
+        total = total + part[:, 512:]
+    score_out[...] = score
+    sim_out[...] = jnp.where(sim > 0.5 * lowest, sim * scale[...] * (1.0 / math.sqrt(total.shape[1])), 0.0)
+    center_out[...] = total * lax.rsqrt(jnp.mean(total * total) + epsilon)
+
+
+def call(kernel, inputs, out_shapes, scratch, flops, mib, scalars=1):
+    return pl.pallas_call(
+        kernel,
+        out_shape=[jax.ShapeDtypeStruct(shape, dtype) for shape, dtype in out_shapes],
+        in_specs=[SMEM] * scalars + [VMEM] * (len(inputs) - scalars),
+        out_specs=[VMEM] * len(out_shapes),
+        scratch_shapes=scratch,
+        compiler_params=pltpu.CompilerParams(vmem_limit_bytes=mib * 1024 * 1024),
+        cost_estimate=pl.CostEstimate(flops=flops, bytes_accessed=8 * 1024 * 1024, transcendentals=0),
+    )(*inputs)
+
+
+def box_shards(embeddings, centroids, cluster, noise_salt):
+    rows_dev, feature_dim = embeddings.shape
+    cent_dev = centroids.shape[0]
+    cent, row = lax.axis_index("cent"), lax.axis_index("rows")
+    layer, core = row // 2, row % 2
+    f32, bf16 = jnp.float32, jnp.bfloat16
+    pos = jnp.stack([cent, row]).astype(jnp.int32)
+    noted = rows_dev + 8
+
+    def along(pairs):
+        return [(2 * a + k, 2 * b + k) for a, b in pairs for k in (0, 1)]
+
+    sibling = [(i, i ^ 1) for i in range(8)]
+    across = along([(1, 2), (2, 1)]) + sibling[0:2] + sibling[6:8]
+    flip = lambda bits: along([(z, z ^ bits) for z in range(4)])
+    by_x, by_y = [(i, i ^ 1) for i in range(4)], [(i, i ^ 2) for i in range(4)]
+    rows = lambda value, pairs: lax.ppermute(value, "rows", pairs)
+    by = lambda value, pairs: lax.ppermute(value, "cent", pairs)
+    together = lax.optimization_barrier
+
+    own, scale = call(
+        note_kernel,
+        [embeddings, cluster.reshape(1, rows_dev)],
+        [((noted, feature_dim), bf16), ((1, rows_dev), f32)],
+        [],
+        rows_dev * feature_dim,
+        16,
+        0,
+    )
+
+    m1, x0, gx, gy = rows(own, across), rows(own, flip(1)), by(own, by_x), by(own, by_y)
+    own_s = rows(own, sibling)
+
+    near_row = jnp.where(layer < 2, 4, 2) + core
+    far_row = jnp.where(layer < 2, 6, 0) + core
+    base = cent * 8
+
+    def ids(devices, count):
+        return jnp.concatenate([device * count + jnp.arange(count, dtype=jnp.int32) for device in devices])
+
+    layer_cents = ids([(cent ^ block) * 8 + (row ^ side) for block in range(4) for side in (0, 1)], cent_dev)
+    visitors = ids([base + row, base + (row ^ 2), base + near_row, base + far_row], rows_dev)
+    noise = lambda row_ids, cent_ids: gumbel_noise(row_ids[None, :], cent_ids[:, None], noise_salt[0])
+    noises = [
+        noise(visitors[:768], layer_cents[:768]),
+        noise(visitors[:768], layer_cents[768:]),
+        noise(visitors[768:], layer_cents),
+    ]
+    m1, x0 = together((m1, x0))
+    m3, x1 = rows(x0, across), rows(m1, flip(1))
+    gx, gy, own_s, m1, x0, *noises = together((gx, gy, own_s, m1, x0, *noises))
+
+    hx = by(jnp.concatenate([centroids, gy[128:]], axis=0), by_x)
+    hy = by(jnp.concatenate([centroids, gx[:128]], axis=0), by_y)
+    gx_s = rows(gx, sibling)
+    half = 4 * rows_dev
+    early = call(
+        early_kernel,
+        [pos, own, own_s, gx, gx_s, x0, m1],
+        [((3, 1, rows_dev), f32), ((8, feature_dim), f32), ((half, 256), f32)],
+        [],
+        2 * 512 * 1024 * feature_dim,
+        16,
+    )
+    m3, x1, hx, hy, gx_s, gy, cents, *early = together((m3, x1, hx, hy, gx_s, gy, centroids, *early))
+
+    x2, d = rows(m3, flip(1)), by(hx[:128], by_y)
+    gy_s, hx_s, hy_s, cents_s = rows(gy, sibling), rows(hx, sibling), rows(hy, sibling), rows(cents, sibling)
+    d_s = by(hy_s[:128], by_x)
+
+    layer_pieces = [own, own_s, gx, gx_s, gy, gy_s, hx, hx_s, hy, hy_s, centroids, cents_s]
+    one_block = [pltpu.VMEM((noted, feature_dim), bf16)]
+    message = ((1, 2 * rows_dev + feature_dim), f32)
+    result, sums, columns = call(
+        first_kernel,
+        [pos] + layer_pieces + [x0, m1, x1, m3, noises[0], noises[2]] + early,
+        [((4, 2, rows_dev), f32), ((8, feature_dim), f32), ((half, 256), f32)],
+        one_block,
+        2 * 256 * 6400 * feature_dim,
+        20,
+    )
+    d, d_s, result = together((d, d_s, result))
+    columns = [early[2], columns]
+    mine, by_one, by_two, by_three = call(
+        second_kernel,
+        [pos, own, x0, m1, x1, m3, d, d_s, noises[1], noises[2], result, sums],
+        [message] * 4,
+        one_block,
+        1,
+        20,
+    )
+    one, two = rows(by_one, flip(1)), rows(by_two, flip(2))
+    x2, by_three = together((x2, by_three))
+    (by_three,) = call(
+        last_kernel,
+        [pos] + layer_pieces + [d, d_s, x2, noises[2]] + columns + [by_three],
+        [message],
+        [],
+        2 * 256 * 3072 * feature_dim,
+        20,
+    )
+    by_three, one, two = together((by_three, one, two))
+    three = rows(by_three, flip(3))
+    score, similar, center = call(
+        final_kernel,
+        [scale, mine, one, two, three],
+        [((1, rows_dev), f32), ((1, rows_dev), f32), ((1, feature_dim), f32)],
+        [],
+        1,
+        4,
+        0,
+    )
+    return (score[0], similar[0], center)
+
+
 def solution(mesh):
-    in_specs = (
-        P(("cent", "rows"), None),
-        P(("cent", "rows"), None),
-        P(("cent", "rows"), None),
-        P(),
-    )
-    out_specs = (P(("cent", "rows")), P(("cent", "rows")), P(("cent", "rows"), None))
-    return jax.shard_map(shards, mesh=mesh, in_specs=in_specs, out_specs=out_specs, check_vma=False)
+    spec = P(("cent", "rows"), None)
+    in_specs = (spec, spec, spec, P())
+    out_specs = (P(("cent", "rows")), P(("cent", "rows")), spec)
+    body = box_shards if dict(mesh.shape) == {"cent": 4, "rows": 8} else shards
+    return jax.shard_map(body, mesh=mesh, in_specs=in_specs, out_specs=out_specs, check_vma=False)

time: 165 us -> 102 us (0.62)
  waiting for transfers between devices: 92.6 us -> 50.7 us
  Pallas kernels: 0 us -> 23.7 us
  matrix products: 15.3 us -> 0 us
  between operations: 14.8 us -> 1.63 us
  local copies, waits for them, and re-layouts: 13.3 us -> 2.05 us
  blocking collectives: 10.1 us -> 0 us
  starting transfers between devices: 13 us -> 21.1 us
    all_to_all x3 -> x0, waiting for transfers between devices: 57.5 us -> none  [the longest x1 49.7 us: shards(): lax.all_to_all(outgoing.reshape(devices, capacity, feature_dim), ('cent',...]
    ppermute x0 -> x20, waiting for transfers between devices: none -> 50.7 us  [the longest x14 27.4 us: box_shards(): rows = lambda value, pairs: lax.ppermute(value, 'rows', pairs)]
    all_gather x2 -> x0, waiting for transfers between devices: 33.7 us -> none  [the longest x1 33.7 us: shards(): piece = lax.all_gather(centroids, 'rows', axis=0, tiled=True)]
    pallas_call x0 -> x6, Pallas kernels: none -> 23.7 us  [call(): pl.pallas_call(kernel, out_shape=[jax.ShapeDtypeStruct(shape, dtype) for...]
    ppermute x0 -> x20, starting transfers between devices: none -> 21.1 us  [the longest x14 13 us: box_shards(): rows = lambda value, pairs: lax.ppermute(value, 'rows', pairs)]
    dot_general x3 -> x0, matrix products: 15.3 us -> none  [the longest x2 13.9 us: step(): lax.dot_general(group, tile, (((1,), (1,)), ((), ())), preferred_element_...]
    all_to_all x3 -> x0, starting transfers between devices: 13 us -> none  [the longest x1 7.3 us: shards(): lax.all_to_all(present.reshape(devices, capacity), ('cent', 'rows'), spli...]
    pmax x1 -> x0, blocking collectives: 10.1 us -> none  [shards(): merged = lax.pmax(result, 'cent')]
  transfers between devices with their start and end apart: 5 -> 20, of which waited for: 4 -> 10; matrix products, arithmetic and copies ran while one was open for 10% -> 3% of each run, Pallas kernels for 0% -> 22%
where the time goes in v1:
time: 102 us
  waiting for transfers between devices  50.7 us (50%)
  Pallas kernels  23.7 us (23%)
  starting transfers between devices  21.1 us (21%)
  other arithmetic  3.04 us (3%)
  local copies, waits for them, and re-layouts  2.05 us (2%)
  between operations  1.63 us (2%)
    ppermute x14, waiting for transfers between devices, box_shards(): rows = lambda value, pairs: lax.ppermute(value, 'rows', pairs)  27.4 us
    pallas_call x6, Pallas kernels, call(): pl.pallas_call(kernel, out_shape=[jax.ShapeDtypeStruct(shape, dtype) for...  23.7 us
    ppermute x6, waiting for transfers between devices, box_shards(): by = lambda value, pairs: lax.ppermute(value, 'cent', pairs)  23.3 us
    ppermute x14, starting transfers between devices, box_shards(): rows = lambda value, pairs: lax.ppermute(value, 'rows', pairs)  13 us
    ppermute x6, starting transfers between devices, box_shards(): by = lambda value, pairs: lax.ppermute(value, 'cent', pairs)  8.05 us
    neg x3, other arithmetic, gumbel_noise(): return -jnp.log(-jnp.log(uniform))  2.67 us
  transfers between devices with their start and end apart: 20, of which 10 were waited for; matrix products, arithmetic and copies ran while one was open for 3% of the time, Pallas kernels for 22%

profile of v1, /device:TPU:0, one launch (start us, length us, event | category | flops | bytes accessed | tf_op | source)
XLA Modules:
  0.0 102.2 jit_solution(6084071903233952996)
XLA Ops:
  0.6 1.2 %copy-done.1 = bf16[256,2048]{1,0:T(8,128)(2,1)S(1)} copy-done((bf16[256,2048]{1,0:T(8,128)(2,1)S(1)}, bf16[256,2048]{1,0:T(8,128)(2,1)}, u32[]{:S(2)}) %copy-start.1) | copy-done | bytes 1048600
  1.9 0.7 copy-done.2
  2.9 0.5 collective-permute-start.3
  3.5 4.1 %collective-permute-start.4 = (bf16[264,2048]{1,0:T(8,128)(2,1)S(1)}, bf16[264,2048]{1,0:T(8,128)(2,1)}, u32[]{:S(2)}, u32[]{:S(2)}) collective-permute-start(bf16[264,2048]{1,0:T(8,128)(2,1)S(1)} %get-tuple-element.47.own.refs_1_), channel_id=1, source_target_pairs={{0,2},{1,3},{2,0},{3,1},{4,6},{5,7},{6,4},{7,5},{8,10},{9,11},{10,... | collective-permute-start | bytes 3244040 | tf_op jit(solution)/shard_map/ppermute | solution.py:362
  7.6 1.5 %collective-permute-start = (bf16[264,2048]{1,0:T(8,128)(2,1)S(1)}, bf16[264,2048]{1,0:T(8,128)(2,1)S(1)}, u32[]{:S(2)}, u32[]{:S(2)}) collective-permute-start(bf16[264,2048]{1,0:T(8,128)(2,1)S(1)} %get-tuple-element.47.own.refs_1_), channel_id=1, source_target_pairs={{0,8},{8,0},{16,24},{24,16},{1,9},{9,1},{17,25},{25,17},{2,10},{10... | collective-permute-start | bytes 3244040 | tf_op jit(solution)/shard_map/ppermute | solution.py:363
  9.1 1.5 %collective-permute-start.1 = (bf16[264,2048]{1,0:T(8,128)(2,1)S(1)}, bf16[264,2048]{1,0:T(8,128)(2,1)S(1)}, u32[]{:S(2)}, u32[]{:S(2)}) collective-permute-start(bf16[264,2048]{1,0:T(8,128)(2,1)S(1)} %get-tuple-element.47.own.refs_1_), channel_id=1, source_target_pairs={{0,16},{8,24},{16,0},{24,8},{1,17},{9,25},{17,1},{25,9},{2,18},{10... | collective-permute-start | bytes 3244040 | tf_op jit(solution)/shard_map/ppermute | solution.py:363
  11.6 0.5 fusion.29.noise
  12.1 0.7 fusion.19.noise_far.refs_16_
  12.8 1.4 %fusion.9.noise = f32[768,768]{1,0:T(8,128)S(1)} fusion(s32[]{:T(128)} %bitcast.6, s32[768]{0:T(1024)S(1)} %broadcast_multiply_fusion.1, s32[768]{0:T(1024)S(1)} %add_multiply_fusion), kind=kLoop, calls=%fused_computation.12 | loop fusion | flops 9437184 | bytes 2365444 | tf_op jit(solution)/shard_map/neg | solution.py:27
  14.3 17.0 %collective-permute-done.4.x0 = bf16[264,2048]{1,0:T(8,128)(2,1)} collective-permute-done((bf16[264,2048]{1,0:T(8,128)(2,1)S(1)}, bf16[264,2048]{1,0:T(8,128)(2,1)}, u32[]{:S(2)}, u32[]{:S(2)}) %collective-permute-start.4) | collective-permute-done | bytes 1081376 | tf_op jit(solution)/shard_map/ppermute | solution.py:362
  31.3 1.4 %collective-permute-done.gx.refs_3_ = bf16[264,2048]{1,0:T(8,128)(2,1)S(1)} collective-permute-done((bf16[264,2048]{1,0:T(8,128)(2,1)S(1)}, bf16[264,2048]{1,0:T(8,128)(2,1)S(1)}, u32[]{:S(2)}, u32[]{:S(2)}) %collective-permute-start) | collective-permute-done | bytes 1081376 | tf_op jit(solution)/shard_map/ppermute | solution.py:363
  32.6 1.2 %collective-permute-done.1.gy.refs_5_ = bf16[264,2048]{1,0:T(8,128)(2,1)S(1)} collective-permute-done((bf16[264,2048]{1,0:T(8,128)(2,1)S(1)}, bf16[264,2048]{1,0:T(8,128)(2,1)S(1)}, u32[]{:S(2)}, u32[]{:S(2)}) %collective-permute-start.1) | collective-permute-done | bytes 1081376 | tf_op jit(solution)/shard_map/ppermute | solution.py:363
  33.9 0.6 collective-permute-start.5
  34.5 2.0 %collective-permute-start.6 = (bf16[264,2048]{1,0:T(8,128)(2,1)}, bf16[264,2048]{1,0:T(8,128)(2,1)S(1)}, u32[]{:S(2)}, u32[]{:S(2)}) collective-permute-start(bf16[264,2048]{1,0:T(8,128)(2,1)} %collective-permute-done.3.m1), channel_id=1, source_target_pairs={{0,2},{1,3},{2,0},{3,1},{4,6},{5,7},{6,4},{7,5},{8,10},{9,11},{10,... | collective-permute-start | bytes 3244040 | tf_op jit(solution)/shard_map/ppermute | solution.py:362
  36.7 0.6 collective-permute-start.7
  37.3 1.6 %collective-permute-start.8 = (bf16[256,2048]{1,0:T(8,128)(2,1)S(1)}, bf16[256,2048]{1,0:T(8,128)(2,1)S(1)}, u32[]{:S(2)}, u32[]{:S(2)}) collective-permute-start(bf16[256,2048]{1,0:T(8,128)(2,1)S(1)} %pad_maximum_fusion.1), channel_id=1, source_target_pairs={{0,16},{8,24},{16,0},{24,8},{1,17},{9,25},{17,1},{25,9},{2,18},{10... | collective-permute-start | bytes 3145736 | tf_op jit(solution)/shard_map/ppermute | solution.py:363
  39.0 5.0 %shard_map.68 = (f32[3,1,256]{2,1,0:T(1,128)S(1)}, f32[8,2048]{1,0:T(8,128)S(1)}, f32[1024,256]{1,0:T(8,128)S(1)}) custom-call(s32[2]{0:T(128)S(1)} %pad_add_fusion.pos.refs_0_, bf16[264,2048]{1,0:T(8,128)(2,1)S(1)} %get-tuple-element.47.own.refs_1_, bf16[264,2048]{1,0:T(8,128)(2,1)} %collective-permute-done.2.own_s.refs_2_, ...), custom_call_target="tpu_custom_call" | custom-call | flops 2147483648 | bytes 8388608 | tf_op jit(solution)/shard_map/pallas_call | solution.py:335
  44.0 18.1 %collective-permute-done.8.hy.refs_9_ = bf16[256,2048]{1,0:T(8,128)(2,1)S(1)} collective-permute-done((bf16[256,2048]{1,0:T(8,128)(2,1)S(1)}, bf16[256,2048]{1,0:T(8,128)(2,1)S(1)}, u32[]{:S(2)}, u32[]{:S(2)}) %collective-permute-start.8) | collective-permute-done | bytes 1048608 | tf_op jit(solution)/shard_map/ppermute | solution.py:363
  62.4 0.5 collective-permute-start.14
  63.8 4.4 %collective-permute-done.11.hy_s.refs_10_ = bf16[256,2048]{1,0:T(8,128)(2,1)S(1)} collective-permute-done((bf16[256,2048]{1,0:T(8,128)(2,1)S(1)}, bf16[256,2048]{1,0:T(8,128)(2,1)S(1)}, u32[]{:S(2)}, u32[]{:S(2)}) %collective-permute-start.11) | collective-permute-done | bytes 1048608 | tf_op jit(solution)/shard_map/ppermute | solution.py:362
  68.2 1.5 %collective-permute-start.10 = (bf16[128,2048]{1,0:T(8,128)(2,1)S(1)}, bf16[128,2048]{1,0:T(8,128)(2,1)S(1)}, u32[]{:S(2)}, u32[]{:S(2)}) collective-permute-start(bf16[128,2048]{1,0:T(8,128)(2,1)S(1)} %slice.21), channel_id=1, source_target_pairs={{0,16},{8,24},{16,0},{24,8},{1,17},{9,25},{17,1},{25,9},{2,18},{10... | collective-permute-start | bytes 1572872 | tf_op jit(solution)/shard_map/ppermute | solution.py:363
  69.8 1.3 %collective-permute-start.12 = (bf16[128,2048]{1,0:T(8,128)(2,1)S(1)}, bf16[128,2048]{1,0:T(8,128)(2,1)S(1)}, u32[]{:S(2)}, u32[]{:S(2)}) collective-permute-start(bf16[128,2048]{1,0:T(8,128)(2,1)S(1)} %slice.23), channel_id=1, source_target_pairs={{0,8},{8,0},{16,24},{24,16},{1,9},{9,1},{17,25},{25,17},{2,10},{10... | collective-permute-start | bytes 1572872 | tf_op jit(solution)/shard_map/ppermute | solution.py:363
  71.1 10.1 %shard_map.69 = (f32[4,2,256]{2,1,0:T(2,128)S(1)}, f32[8,2048]{1,0:T(8,128)S(1)}, f32[1024,256]{1,0:T(8,128)S(1)}) custom-call(s32[2]{0:T(128)S(1)} %pad_add_fusion.pos.refs_0_, bf16[264,2048]{1,0:T(8,128)(2,1)S(1)} %get-tuple-element.47.own.refs_1_, bf16[264,2048]{1,0:T(8,128)(2,1)} %collective-permute-done.2.own_s.refs_2_, ...), custom_call_target="tpu_custom_call" | custom-call | flops 6710886400 | bytes 8388608 | tf_op jit(solution)/shard_map/pallas_call | solution.py:335
  81.2 0.9 collective-permute-done.10.d.refs_13_
  82.2 1.4 %collective-permute-done.12.d_s.refs_14_ = bf16[128,2048]{1,0:T(8,128)(2,1)S(1)} collective-permute-done((bf16[128,2048]{1,0:T(8,128)(2,1)S(1)}, bf16[128,2048]{1,0:T(8,128)(2,1)S(1)}, u32[]{:S(2)}, u32[]{:S(2)}) %collective-permute-start.12) | collective-permute-done | bytes 524320 | tf_op jit(solution)/shard_map/ppermute | solution.py:363
  83.5 2.7 %shard_map.70 = (f32[1,2560]{1,0:T(1,128)S(1)}, f32[1,2560]{1,0:T(1,128)S(1)}, f32[1,2560]{1,0:T(1,128)S(1)}, f32[1,2560]{1,0:T(1,128)S(1)}) custom-call(s32[2]{0:T(128)S(1)} %pad_add_fusion.pos.refs_0_, bf16[264,2048]{1,0:T(8,128)(2,1)S(1)} %get-tuple-element.47.own.refs_1_, bf16[264,2048]{1,0:T(8,128)(2,1)} %collective-permute-done.4.x0, ...), custom_call_target="tpu_custom_call" | custom-call | flops 1 | bytes 8388608 | tf_op jit(solution)/shard_map/pallas_call | solution.py:335
  86.2 3.1 %collective-permute-done.16.refs_15_ = bf16[264,2048]{1,0:T(8,128)(2,1)S(1)} collective-permute-done((bf16[264,2048]{1,0:T(8,128)(2,1)S(1)}, bf16[264,2048]{1,0:T(8,128)(2,1)S(1)}, u32[]{:S(2)}, u32[]{:S(2)}) %collective-permute-start.16) | collective-permute-done | bytes 1081376 | tf_op jit(solution)/shard_map/ppermute | solution.py:362
  89.6 1.5 %collective-permute-start.18 = (f32[1,2560]{1,0:T(1,128)S(1)}, f32[1,2560]{1,0:T(1,128)S(1)}, u32[]{:S(2)}, u32[]{:S(2)}) collective-permute-start(f32[1,2560]{1,0:T(1,128)S(1)} %get-tuple-element.82), channel_id=1, source_target_pairs={{0,4},{1,5},{2,6},{3,7},{4,0},{5,1},{6,2},{7,3},{8,12},{9,13},{10,... | collective-permute-start | bytes 30728 | tf_op jit(solution)/shard_map/ppermute | solution.py:362
  91.1 4.7 %shard_map.71 = f32[1,2560]{1,0:T(1,128)S(1)} custom-call(s32[2]{0:T(128)S(1)} %pad_add_fusion.pos.refs_0_, bf16[264,2048]{1,0:T(8,128)(2,1)S(1)} %get-tuple-element.47.own.refs_1_, bf16[264,2048]{1,0:T(8,128)(2,1)} %collective-permute-done.2.own_s.refs_2_, bf16[264,2048]{1,0:T(8,128)(2,1)S(1)} %collective-permute-done.gx.refs_3_, ...), custom_call_target="tpu_custom_call" | custom-call | flops 3221225472 | bytes 8388608 | tf_op jit(solution)/shard_map/pallas_call | solution.py:335
  95.9 2.6 %collective-permute-start.19 = (f32[1,2560]{1,0:T(1,128)S(1)}, f32[1,2560]{1,0:T(1,128)S(1)}, u32[]{:S(2)}, u32[]{:S(2)}) collective-permute-start(f32[1,2560]{1,0:T(1,128)S(1)} %shard_map.71), channel_id=1, source_target_pairs={{0,6},{1,7},{2,4},{3,5},{4,2},{5,3},{6,0},{7,1},{8,14},{9,15},{10,... | collective-permute-start | bytes 30728 | tf_op jit(solution)/shard_map/ppermute | solution.py:362
  98.5 2.9 %collective-permute-done.19.refs_3_ = f32[1,2560]{1,0:T(1,128)S(1)} collective-permute-done((f32[1,2560]{1,0:T(1,128)S(1)}, f32[1,2560]{1,0:T(1,128)S(1)}, u32[]{:S(2)}, u32[]{:S(2)}) %collective-permute-start.19) | collective-permute-done | bytes 10272 | tf_op jit(solution)/shard_map/ppermute | solution.py:362
  101.4 0.8 shard_map.72
  (53 shorter events, 2.3 us)
Async XLA Ops:
  0.6 1.2 %copy-start.1 = (bf16[256,2048]{1,0:T(8,128)(2,1)S(1)}, bf16[256,2048]{1,0:T(8,128)(2,1)}, u32[]{:S(2)}) copy-start(bf16[256,2048]{1,0:T(8,128)(2,1)} %emb.1) | copy-start | bytes 3145732
  1.9 0.7 copy-start.2
  2.9 11.4 %collective-permute-start.3 = (bf16[264,2048]{1,0:T(8,128)(2,1)S(1)}, bf16[264,2048]{1,0:T(8,128)(2,1)}, u32[]{:S(2)}, u32[]{:S(2)}) collective-permute-start(bf16[264,2048]{1,0:T(8,128)(2,1)S(1)} %get-tuple-element.47.own.refs_1_), channel_id=1, source_target_pairs={{2,4},{3,5},{4,2},{5,3},{0,1},{1,0},{6,7},{7,6},{10,12},{11,13},{1... | collective-permute-start | bytes 3244040 | tf_op jit(solution)/shard_map/ppermute | solution.py:362
  3.5 27.8 %collective-permute-start.4 = (bf16[264,2048]{1,0:T(8,128)(2,1)S(1)}, bf16[264,2048]{1,0:T(8,128)(2,1)}, u32[]{:S(2)}, u32[]{:S(2)}) collective-permute-start(bf16[264,2048]{1,0:T(8,128)(2,1)S(1)} %get-tuple-element.47.own.refs_1_), channel_id=1, source_target_pairs={{0,2},{1,3},{2,0},{3,1},{4,6},{5,7},{6,4},{7,5},{8,10},{9,11},{10,... | collective-permute-start | bytes 3244040 | tf_op jit(solution)/shard_map/ppermute | solution.py:362
  7.6 25.0 %collective-permute-start = (bf16[264,2048]{1,0:T(8,128)(2,1)S(1)}, bf16[264,2048]{1,0:T(8,128)(2,1)S(1)}, u32[]{:S(2)}, u32[]{:S(2)}) collective-permute-start(bf16[264,2048]{1,0:T(8,128)(2,1)S(1)} %get-tuple-element.47.own.refs_1_), channel_id=1, source_target_pairs={{0,8},{8,0},{16,24},{24,16},{1,9},{9,1},{17,25},{25,17},{2,10},{10... | collective-permute-start | bytes 3244040 | tf_op jit(solution)/shard_map/ppermute | solution.py:363
  9.1 24.8 %collective-permute-start.1 = (bf16[264,2048]{1,0:T(8,128)(2,1)S(1)}, bf16[264,2048]{1,0:T(8,128)(2,1)S(1)}, u32[]{:S(2)}, u32[]{:S(2)}) collective-permute-start(bf16[264,2048]{1,0:T(8,128)(2,1)S(1)} %get-tuple-element.47.own.refs_1_), channel_id=1, source_target_pairs={{0,16},{8,24},{16,0},{24,8},{1,17},{9,25},{17,1},{25,9},{2,18},{10... | collective-permute-start | bytes 3244040 | tf_op jit(solution)/shard_map/ppermute | solution.py:363
  10.6 23.2 %collective-permute-start.2 = (bf16[264,2048]{1,0:T(8,128)(2,1)S(1)}, bf16[264,2048]{1,0:T(8,128)(2,1)}, u32[]{:S(2)}, u32[]{:S(2)}) collective-permute-start(bf16[264,2048]{1,0:T(8,128)(2,1)S(1)} %get-tuple-element.47.own.refs_1_), channel_id=1, source_target_pairs={{0,1},{1,0},{2,3},{3,2},{4,5},{5,4},{6,7},{7,6},{8,9},{9,8},{10,11... | collective-permute-start | bytes 3244040 | tf_op jit(solution)/shard_map/ppermute | solution.py:362
  12.8 23.7 %copy-start = (bf16[128,2048]{1,0:T(8,128)(2,1)S(1)}, bf16[128,2048]{1,0:T(8,128)(2,1)}, u32[]{:S(2)}) copy-start(bf16[128,2048]{1,0:T(8,128)(2,1)} %refs_11_.1) | copy-start | bytes 1572868
  33.9 5.2 %collective-permute-start.9 = (bf16[264,2048]{1,0:T(8,128)(2,1)S(1)}, bf16[264,2048]{1,0:T(8,128)(2,1)S(1)}, u32[]{:S(2)}, u32[]{:S(2)}) collective-permute-start(bf16[264,2048]{1,0:T(8,128)(2,1)S(1)} %collective-permute-done.gx.refs_3_), channel_id=1, source_target_pairs={{0,1},{1,0},{2,3},{3,2},{4,5},{5,4},{6,7},{7,6},{8,9},{9,8},{10,11... | collective-permute-start | bytes 3244040 | tf_op jit(solution)/shard_map/ppermute | solution.py:362
  33.9 28.5 %collective-permute-start.5 = (bf16[264,2048]{1,0:T(8,128)(2,1)}, bf16[264,2048]{1,0:T(8,128)(2,1)S(1)}, u32[]{:S(2)}, u32[]{:S(2)}) collective-permute-start(bf16[264,2048]{1,0:T(8,128)(2,1)} %collective-permute-done.4.x0), channel_id=1, source_target_pairs={{2,4},{3,5},{4,2},{5,3},{0,1},{1,0},{6,7},{7,6},{10,12},{11,13},{1... | collective-permute-start | bytes 3244040 | tf_op jit(solution)/shard_map/ppermute | solution.py:362
  34.5 28.0 %collective-permute-start.6 = (bf16[264,2048]{1,0:T(8,128)(2,1)}, bf16[264,2048]{1,0:T(8,128)(2,1)S(1)}, u32[]{:S(2)}, u32[]{:S(2)}) collective-permute-start(bf16[264,2048]{1,0:T(8,128)(2,1)} %collective-permute-done.3.m1), channel_id=1, source_target_pairs={{0,2},{1,3},{2,0},{3,1},{4,6},{5,7},{6,4},{7,5},{8,10},{9,11},{10,... | collective-permute-start | bytes 3244040 | tf_op jit(solution)/shard_map/ppermute | solution.py:362
  36.7 25.8 %collective-permute-start.7 = (bf16[264,2048]{1,0:T(8,128)(2,1)S(1)}, bf16[264,2048]{1,0:T(8,128)(2,1)S(1)}, u32[]{:S(2)}, u32[]{:S(2)}) collective-permute-start(bf16[264,2048]{1,0:T(8,128)(2,1)S(1)} %pad_maximum_fusion), channel_id=1, source_target_pairs={{0,8},{8,0},{16,24},{24,16},{1,9},{9,1},{17,25},{25,17},{2,10},{10... | collective-permute-start | bytes 3244040 | tf_op jit(solution)/shard_map/ppermute | solution.py:363
  37.3 24.8 %collective-permute-start.8 = (bf16[256,2048]{1,0:T(8,128)(2,1)S(1)}, bf16[256,2048]{1,0:T(8,128)(2,1)S(1)}, u32[]{:S(2)}, u32[]{:S(2)}) collective-permute-start(bf16[256,2048]{1,0:T(8,128)(2,1)S(1)} %pad_maximum_fusion.1), channel_id=1, source_target_pairs={{0,16},{8,24},{16,0},{24,8},{1,17},{9,25},{17,1},{25,9},{2,18},{10... | collective-permute-start | bytes 3145736 | tf_op jit(solution)/shard_map/ppermute | solution.py:363
  62.4 8.7 %collective-permute-start.13 = (bf16[264,2048]{1,0:T(8,128)(2,1)S(1)}, bf16[264,2048]{1,0:T(8,128)(2,1)S(1)}, u32[]{:S(2)}, u32[]{:S(2)}) collective-permute-start(bf16[264,2048]{1,0:T(8,128)(2,1)S(1)} %collective-permute-done.1.gy.refs_5_), channel_id=1, source_target_pairs={{0,1},{1,0},{2,3},{3,2},{4,5},{5,4},{6,7},{7,6},{8,9},{9,8},{10,11... | collective-permute-start | bytes 3244040 | tf_op jit(solution)/shard_map/ppermute | solution.py:362
  62.4 8.7 %collective-permute-start.14 = (bf16[264,2048]{1,0:T(8,128)(2,1)S(1)}, bf16[264,2048]{1,0:T(8,128)(2,1)S(1)}, u32[]{:S(2)}, u32[]{:S(2)}) collective-permute-start(bf16[264,2048]{1,0:T(8,128)(2,1)S(1)} %collective-permute-done.7.hx.refs_7_), channel_id=1, source_target_pairs={{0,1},{1,0},{2,3},{3,2},{4,5},{5,4},{6,7},{7,6},{8,9},{9,8},{10,11... | collective-permute-start | bytes 3244040 | tf_op jit(solution)/shard_map/ppermute | solution.py:362
  62.9 5.2 %collective-permute-start.11 = (bf16[256,2048]{1,0:T(8,128)(2,1)S(1)}, bf16[256,2048]{1,0:T(8,128)(2,1)S(1)}, u32[]{:S(2)}, u32[]{:S(2)}) collective-permute-start(bf16[256,2048]{1,0:T(8,128)(2,1)S(1)} %collective-permute-done.8.hy.refs_9_), channel_id=1, source_target_pairs={{0,1},{1,0},{2,3},{3,2},{4,5},{5,4},{6,7},{7,6},{8,9},{9,8},{10,11... | collective-permute-start | bytes 3145736 | tf_op jit(solution)/shard_map/ppermute | solution.py:362
  63.0 6.7 %collective-permute-start.15 = (bf16[128,2048]{1,0:T(8,128)(2,1)S(1)}, bf16[128,2048]{1,0:T(8,128)(2,1)S(1)}, u32[]{:S(2)}, u32[]{:S(2)}) collective-permute-start(bf16[128,2048]{1,0:T(8,128)(2,1)S(1)} %copy-done), channel_id=1, source_target_pairs={{0,1},{1,0},{2,3},{3,2},{4,5},{5,4},{6,7},{7,6},{8,9},{9,8},{10,11... | collective-permute-start | bytes 1572872 | tf_op jit(solution)/shard_map/ppermute | solution.py:362
  63.5 25.8 %collective-permute-start.16 = (bf16[264,2048]{1,0:T(8,128)(2,1)S(1)}, bf16[264,2048]{1,0:T(8,128)(2,1)S(1)}, u32[]{:S(2)}, u32[]{:S(2)}) collective-permute-start(bf16[264,2048]{1,0:T(8,128)(2,1)S(1)} %collective-permute-done.5.m3), channel_id=1, source_target_pairs={{0,2},{1,3},{2,0},{3,1},{4,6},{5,7},{6,4},{7,5},{8,10},{9,11},{10,... | collective-permute-start | bytes 3244040 | tf_op jit(solution)/shard_map/ppermute | solution.py:362
  68.2 14.0 %collective-permute-start.10 = (bf16[128,2048]{1,0:T(8,128)(2,1)S(1)}, bf16[128,2048]{1,0:T(8,128)(2,1)S(1)}, u32[]{:S(2)}, u32[]{:S(2)}) collective-permute-start(bf16[128,2048]{1,0:T(8,128)(2,1)S(1)} %slice.21), channel_id=1, source_target_pairs={{0,16},{8,24},{16,0},{24,8},{1,17},{9,25},{17,1},{25,9},{2,18},{10... | collective-permute-start | bytes 1572872 | tf_op jit(solution)/shard_map/ppermute | solution.py:363
  69.8 13.8 %collective-permute-start.12 = (bf16[128,2048]{1,0:T(8,128)(2,1)S(1)}, bf16[128,2048]{1,0:T(8,128)(2,1)S(1)}, u32[]{:S(2)}, u32[]{:S(2)}) collective-permute-start(bf16[128,2048]{1,0:T(8,128)(2,1)S(1)} %slice.23), channel_id=1, source_target_pairs={{0,8},{8,0},{16,24},{24,16},{1,9},{9,1},{17,25},{25,17},{2,10},{10... | collective-permute-start | bytes 1572872 | tf_op jit(solution)/shard_map/ppermute | solution.py:363
  89.3 6.6 %collective-permute-start.17 = (f32[1,2560]{1,0:T(1,128)S(1)}, f32[1,2560]{1,0:T(1,128)S(1)}, u32[]{:S(2)}, u32[]{:S(2)}) collective-permute-start(f32[1,2560]{1,0:T(1,128)S(1)} %get-tuple-element.81), channel_id=1, source_target_pairs={{0,2},{1,3},{2,0},{3,1},{4,6},{5,7},{6,4},{7,5},{8,10},{9,11},{10,... | collective-permute-start | bytes 30728 | tf_op jit(solution)/shard_map/ppermute | solution.py:362
  89.6 6.3 %collective-permute-start.18 = (f32[1,2560]{1,0:T(1,128)S(1)}, f32[1,2560]{1,0:T(1,128)S(1)}, u32[]{:S(2)}, u32[]{:S(2)}) collective-permute-start(f32[1,2560]{1,0:T(1,128)S(1)} %get-tuple-element.82), channel_id=1, source_target_pairs={{0,4},{1,5},{2,6},{3,7},{4,0},{5,1},{6,2},{7,3},{8,12},{9,13},{10,... | collective-permute-start | bytes 30728 | tf_op jit(solution)/shard_map/ppermute | solution.py:362
  95.9 5.5 %collective-permute-start.19 = (f32[1,2560]{1,0:T(1,128)S(1)}, f32[1,2560]{1,0:T(1,128)S(1)}, u32[]{:S(2)}, u32[]{:S(2)}) collective-permute-start(f32[1,2560]{1,0:T(1,128)S(1)} %shard_map.71), channel_id=1, source_target_pairs={{0,6},{1,7},{2,4},{3,5},{4,2},{5,3},{6,0},{7,1},{8,14},{9,15},{10,... | collective-permute-start | bytes 30728 | tf_op jit(solution)/shard_map/ppermute | solution.py:362

commit v2 on v1

--- a/solution.py
+++ b/solution.py
@@ -391,9 +391,8 @@
         noise(visitors[:768], layer_cents[768:]),
         noise(visitors[768:], layer_cents),
     ]
-    m1, x0 = together((m1, x0))
+    m1, x0, *noises = together((m1, x0, *noises))
     m3, x1 = rows(x0, across), rows(m1, flip(1))
-    gx, gy, own_s, m1, x0, *noises = together((gx, gy, own_s, m1, x0, *noises))
 
     hx = by(jnp.concatenate([centroids, gy[128:]], axis=0), by_x)
     hy = by(jnp.concatenate([centroids, gx[:128]], axis=0), by_y)
@@ -407,7 +406,7 @@
         2 * 512 * 1024 * feature_dim,
         16,
     )
-    m3, x1, hx, hy, gx_s, gy, cents, *early = together((m3, x1, hx, hy, gx_s, gy, centroids, *early))
+    m3, x1, gx_s, gy, cents, *early = together((m3, x1, gx_s, gy, centroids, *early))
 
     x2, d = rows(m3, flip(1)), by(hx[:128], by_y)
     gy_s, hx_s, hy_s, cents_s = rows(gy, sibling), rows(hx, sibling), rows(hy, sibling), rows(cents, sibling)
@@ -441,7 +440,7 @@
         [pos] + layer_pieces + [d, d_s, x2, noises[2]] + columns + [by_three],
         [message],
         [],
-        2 * 256 * 3072 * feature_dim,
+        1,
         20,
     )
     by_three, one, two = together((by_three, one, two))

time: 102 us -> 100 us (0.980)
  waiting for transfers between devices: 50.7 us -> 48.1 us
  starting transfers between devices: 21.1 us -> 19.5 us
  local copies, waits for them, and re-layouts: 2.05 us -> 3.08 us
    ppermute x6, waiting for transfers between devices: 23.3 us -> 8.3 us  [box_shards(): by = lambda value, pairs: lax.ppermute(value, 'cent', pairs)]
    ppermute x14, waiting for transfers between devices: 27.4 us -> 39.8 us  [box_shards(): rows = lambda value, pairs: lax.ppermute(value, 'rows', pairs)]
    slice x1, local copies, waits for them, and re-layouts: 0.03 us -> 1.08 us  [box_shards(): hy = by(jnp.concatenate([centroids, gx[:128]], axis=0), by_y)]
  transfers between devices with their start and end apart: 20 -> 20, of which waited for: 10 -> 10; matrix products, arithmetic and copies ran while one was open for 3% -> 4% of each run, Pallas kernels for 22% -> 24%
where the time goes in v2:
time: 100 us
  waiting for transfers between devices  48.1 us (48%)
  Pallas kernels  24.7 us (25%)
  starting transfers between devices  19.5 us (20%)
  local copies, waits for them, and re-layouts  3.08 us (3%)
  other arithmetic  3.05 us (3%)
  between operations  1.6 us (2%)
    ppermute x14, waiting for transfers between devices, box_shards(): rows = lambda value, pairs: lax.ppermute(value, 'rows', pairs)  39.8 us
    pallas_call x6, Pallas kernels, call(): pl.pallas_call(kernel, out_shape=[jax.ShapeDtypeStruct(shape, dtype) for...  24.7 us
    ppermute x14, starting transfers between devices, box_shards(): rows = lambda value, pairs: lax.ppermute(value, 'rows', pairs)  12 us
    ppermute x6, waiting for transfers between devices, box_shards(): by = lambda value, pairs: lax.ppermute(value, 'cent', pairs)  8.3 us
    ppermute x6, starting transfers between devices, box_shards(): by = lambda value, pairs: lax.ppermute(value, 'cent', pairs)  7.53 us
    neg x3, other arithmetic, gumbel_noise(): return -jnp.log(-jnp.log(uniform))  2.67 us
  transfers between devices with their start and end apart: 20, of which 10 were waited for; matrix products, arithmetic and copies ran while one was open for 4% of the time, Pallas kernels for 24%

profile of v2, /device:TPU:0, one launch (start us, length us, event | category | flops | bytes accessed | tf_op | source)
XLA Modules:
  0.0 100.1 jit_solution(17859559425366408636)
XLA Ops:
  0.6 1.2 %copy-done.1 = bf16[256,2048]{1,0:T(8,128)(2,1)S(1)} copy-done((bf16[256,2048]{1,0:T(8,128)(2,1)S(1)}, bf16[256,2048]{1,0:T(8,128)(2,1)}, u32[]{:S(2)}) %copy-start.1) | copy-done | bytes 1048600
  1.9 0.7 copy-done.2
  3.5 4.1 %collective-permute-start.1 = (bf16[264,2048]{1,0:T(8,128)(2,1)S(1)}, bf16[264,2048]{1,0:T(8,128)(2,1)}, u32[]{:S(2)}, u32[]{:S(2)}) collective-permute-start(bf16[264,2048]{1,0:T(8,128)(2,1)S(1)} %get-tuple-element.40.own.refs_1_), channel_id=1, source_target_pairs={{0,2},{1,3},{2,0},{3,1},{4,6},{5,7},{6,4},{7,5},{8,10},{9,11},{10,... | collective-permute-start | bytes 3244040 | tf_op jit(solution)/shard_map/ppermute | solution.py:362
  7.6 1.5 %collective-permute-start.4 = (bf16[264,2048]{1,0:T(8,128)(2,1)S(1)}, bf16[264,2048]{1,0:T(8,128)(2,1)}, u32[]{:S(2)}, u32[]{:S(2)}) collective-permute-start(bf16[264,2048]{1,0:T(8,128)(2,1)S(1)} %get-tuple-element.40.own.refs_1_), channel_id=1, source_target_pairs={{0,8},{8,0},{16,24},{24,16},{1,9},{9,1},{17,25},{25,17},{2,10},{10... | collective-permute-start | bytes 3244040 | tf_op jit(solution)/shard_map/ppermute | solution.py:363
  9.1 1.5 %collective-permute-start.6 = (bf16[264,2048]{1,0:T(8,128)(2,1)S(1)}, bf16[264,2048]{1,0:T(8,128)(2,1)S(1)}, u32[]{:S(2)}, u32[]{:S(2)}) collective-permute-start(bf16[264,2048]{1,0:T(8,128)(2,1)S(1)} %get-tuple-element.40.own.refs_1_), channel_id=1, source_target_pairs={{0,16},{8,24},{16,0},{24,8},{1,17},{9,25},{17,1},{25,9},{2,18},{10... | collective-permute-start | bytes 3244040 | tf_op jit(solution)/shard_map/ppermute | solution.py:363
  11.5 0.5 fusion.29.noise
  12.1 0.7 fusion.19.noise_far.refs_16_
  12.8 1.4 %fusion.9.noise = f32[768,768]{1,0:T(8,128)S(1)} fusion(s32[]{:T(128)} %bitcast.6, s32[768]{0:T(1024)S(1)} %broadcast_multiply_fusion.1, s32[768]{0:T(1024)S(1)} %add_multiply_fusion), kind=kLoop, calls=%fused_computation.12 | loop fusion | flops 9437184 | bytes 2365444 | tf_op jit(solution)/shard_map/neg | solution.py:27
  14.3 17.0 %collective-permute-done.1.x0 = bf16[264,2048]{1,0:T(8,128)(2,1)} collective-permute-done((bf16[264,2048]{1,0:T(8,128)(2,1)S(1)}, bf16[264,2048]{1,0:T(8,128)(2,1)}, u32[]{:S(2)}, u32[]{:S(2)}) %collective-permute-start.1) | collective-permute-done | bytes 1081376 | tf_op jit(solution)/shard_map/ppermute | solution.py:362
  31.3 2.5 %collective-permute-start.3 = (bf16[264,2048]{1,0:T(8,128)(2,1)}, bf16[264,2048]{1,0:T(8,128)(2,1)S(1)}, u32[]{:S(2)}, u32[]{:S(2)}) collective-permute-start(bf16[264,2048]{1,0:T(8,128)(2,1)} %collective-permute-done.m1), channel_id=1, source_target_pairs={{0,2},{1,3},{2,0},{3,1},{4,6},{5,7},{6,4},{7,5},{8,10},{9,11},{10,... | collective-permute-start | bytes 3244040 | tf_op jit(solution)/shard_map/ppermute | solution.py:362
  33.8 1.5 %collective-permute-done.6.gy.refs_5_ = bf16[264,2048]{1,0:T(8,128)(2,1)S(1)} collective-permute-done((bf16[264,2048]{1,0:T(8,128)(2,1)S(1)}, bf16[264,2048]{1,0:T(8,128)(2,1)S(1)}, u32[]{:S(2)}, u32[]{:S(2)}) %collective-permute-start.6) | collective-permute-done | bytes 1081376 | tf_op jit(solution)/shard_map/ppermute | solution.py:363
  35.5 0.6 collective-permute-start.8
  36.1 1.1 %slice.25 = bf16[128,2048]{1,0:T(8,128)(2,1)S(1)} slice(bf16[264,2048]{1,0:T(8,128)(2,1)} %collective-permute-done.4.gx.refs_3_), slice={[0:128], [0:2048]} | slice | bytes 1048576 | tf_op jit(solution)/shard_map/slice | solution.py:398
  37.3 1.6 %collective-permute-start.10 = (bf16[256,2048]{1,0:T(8,128)(2,1)S(1)}, bf16[256,2048]{1,0:T(8,128)(2,1)S(1)}, u32[]{:S(2)}, u32[]{:S(2)}) collective-permute-start(bf16[256,2048]{1,0:T(8,128)(2,1)S(1)} %pad_maximum_fusion.1), channel_id=1, source_target_pairs={{0,16},{8,24},{16,0},{24,8},{1,17},{9,25},{17,1},{25,9},{2,18},{10... | collective-permute-start | bytes 3145736 | tf_op jit(solution)/shard_map/ppermute | solution.py:363
  39.0 5.3 %shard_map.68 = (f32[3,1,256]{2,1,0:T(1,128)S(1)}, f32[8,2048]{1,0:T(8,128)S(1)}, f32[1024,256]{1,0:T(8,128)S(1)}) custom-call(s32[2]{0:T(128)S(1)} %pad_add_fusion.pos.refs_0_, bf16[264,2048]{1,0:T(8,128)(2,1)S(1)} %get-tuple-element.40.own.refs_1_, bf16[264,2048]{1,0:T(8,128)(2,1)} %collective-permute-done.7.own_s.refs_2_, ...), custom_call_target="tpu_custom_call" | custom-call | flops 2147483648 | bytes 8388608 | tf_op jit(solution)/shard_map/pallas_call | solution.py:335
  44.3 13.5 %collective-permute-done.3.x1 = bf16[264,2048]{1,0:T(8,128)(2,1)S(1)} collective-permute-done((bf16[264,2048]{1,0:T(8,128)(2,1)}, bf16[264,2048]{1,0:T(8,128)(2,1)S(1)}, u32[]{:S(2)}, u32[]{:S(2)}) %collective-permute-start.3) | collective-permute-done | bytes 1081376 | tf_op jit(solution)/shard_map/ppermute | solution.py:362
  57.8 3.3 %collective-permute-done.8.hx.refs_7_ = bf16[264,2048]{1,0:T(8,128)(2,1)S(1)} collective-permute-done((bf16[264,2048]{1,0:T(8,128)(2,1)S(1)}, bf16[264,2048]{1,0:T(8,128)(2,1)S(1)}, u32[]{:S(2)}, u32[]{:S(2)}) %collective-permute-start.8) | collective-permute-done | bytes 1081376 | tf_op jit(solution)/shard_map/ppermute | solution.py:363
  61.1 1.0 collective-permute-done.10.hy.refs_9_
  62.6 2.7 %collective-permute-done.11.hy_s.refs_10_ = bf16[256,2048]{1,0:T(8,128)(2,1)S(1)} collective-permute-done((bf16[256,2048]{1,0:T(8,128)(2,1)S(1)}, bf16[256,2048]{1,0:T(8,128)(2,1)S(1)}, u32[]{:S(2)}, u32[]{:S(2)}) %collective-permute-start.11) | collective-permute-done | bytes 1048608 | tf_op jit(solution)/shard_map/ppermute | solution.py:362
  65.3 1.5 %collective-permute-start.9 = (bf16[128,2048]{1,0:T(8,128)(2,1)S(1)}, bf16[128,2048]{1,0:T(8,128)(2,1)S(1)}, u32[]{:S(2)}, u32[]{:S(2)}) collective-permute-start(bf16[128,2048]{1,0:T(8,128)(2,1)S(1)} %slice.24), channel_id=1, source_target_pairs={{0,16},{8,24},{16,0},{24,8},{1,17},{9,25},{17,1},{25,9},{2,18},{10... | collective-permute-start | bytes 1572872 | tf_op jit(solution)/shard_map/ppermute | solution.py:363
  66.8 0.8 collective-permute-start.12
  67.7 10.5 %shard_map.69 = (f32[4,2,256]{2,1,0:T(2,128)S(1)}, f32[8,2048]{1,0:T(8,128)S(1)}, f32[1024,256]{1,0:T(8,128)S(1)}) custom-call(s32[2]{0:T(128)S(1)} %pad_add_fusion.pos.refs_0_, bf16[264,2048]{1,0:T(8,128)(2,1)S(1)} %get-tuple-element.40.own.refs_1_, bf16[264,2048]{1,0:T(8,128)(2,1)} %collective-permute-done.7.own_s.refs_2_, ...), custom_call_target="tpu_custom_call" | custom-call | flops 6710886400 | bytes 8388608 | tf_op jit(solution)/shard_map/pallas_call | solution.py:335
  78.1 1.1 %collective-permute-done.9.d.refs_13_ = bf16[128,2048]{1,0:T(8,128)(2,1)S(1)} collective-permute-done((bf16[128,2048]{1,0:T(8,128)(2,1)S(1)}, bf16[128,2048]{1,0:T(8,128)(2,1)S(1)}, u32[]{:S(2)}, u32[]{:S(2)}) %collective-permute-start.9) | collective-permute-done | bytes 524320 | tf_op jit(solution)/shard_map/ppermute | solution.py:363
  79.2 1.4 %collective-permute-done.12.d_s.refs_14_ = bf16[128,2048]{1,0:T(8,128)(2,1)S(1)} collective-permute-done((bf16[128,2048]{1,0:T(8,128)(2,1)S(1)}, bf16[128,2048]{1,0:T(8,128)(2,1)S(1)}, u32[]{:S(2)}, u32[]{:S(2)}) %collective-permute-start.12) | collective-permute-done | bytes 524320 | tf_op jit(solution)/shard_map/ppermute | solution.py:363
  80.6 2.7 %shard_map.70 = (f32[1,2560]{1,0:T(1,128)S(1)}, f32[1,2560]{1,0:T(1,128)S(1)}, f32[1,2560]{1,0:T(1,128)S(1)}, f32[1,2560]{1,0:T(1,128)S(1)}) custom-call(s32[2]{0:T(128)S(1)} %pad_add_fusion.pos.refs_0_, bf16[264,2048]{1,0:T(8,128)(2,1)S(1)} %get-tuple-element.40.own.refs_1_, bf16[264,2048]{1,0:T(8,128)(2,1)} %collective-permute-done.1.x0, ...), custom_call_target="tpu_custom_call" | custom-call | flops 1 | bytes 8388608 | tf_op jit(solution)/shard_map/pallas_call | solution.py:335
  83.3 0.6 collective-permute-start.17
  83.8 1.7 %collective-permute-start.18 = (f32[1,2560]{1,0:T(1,128)S(1)}, f32[1,2560]{1,0:T(1,128)S(1)}, u32[]{:S(2)}, u32[]{:S(2)}) collective-permute-start(f32[1,2560]{1,0:T(1,128)S(1)} %get-tuple-element.68), channel_id=1, source_target_pairs={{0,4},{1,5},{2,6},{3,7},{4,0},{5,1},{6,2},{7,3},{8,12},{9,13},{10,... | collective-permute-start | bytes 30728 | tf_op jit(solution)/shard_map/ppermute | solution.py:362
  85.5 3.2 %collective-permute-done.16.refs_15_ = bf16[264,2048]{1,0:T(8,128)(2,1)S(1)} collective-permute-done((bf16[264,2048]{1,0:T(8,128)(2,1)S(1)}, bf16[264,2048]{1,0:T(8,128)(2,1)S(1)}, u32[]{:S(2)}, u32[]{:S(2)}) %collective-permute-start.16) | collective-permute-done | bytes 1081376 | tf_op jit(solution)/shard_map/ppermute | solution.py:362
  88.7 5.1 %shard_map.71 = f32[1,2560]{1,0:T(1,128)S(1)} custom-call(s32[2]{0:T(128)S(1)} %pad_add_fusion.pos.refs_0_, bf16[264,2048]{1,0:T(8,128)(2,1)S(1)} %get-tuple-element.40.own.refs_1_, bf16[264,2048]{1,0:T(8,128)(2,1)} %collective-permute-done.7.own_s.refs_2_, bf16[264,2048]{1,0:T(8,128)(2,1)} %collective-permute-done.4.gx.refs_3_, ...), custom_call_target="tpu_custom_call" | custom-call | flops 1 | bytes 8388608 | tf_op jit(solution)/shard_map/pallas_call | solution.py:335
  93.8 2.1 %collective-permute-start.19 = (f32[1,2560]{1,0:T(1,128)S(1)}, f32[1,2560]{1,0:T(1,128)S(1)}, u32[]{:S(2)}, u32[]{:S(2)}) collective-permute-start(f32[1,2560]{1,0:T(1,128)S(1)} %shard_map.71), channel_id=1, source_target_pairs={{0,6},{1,7},{2,4},{3,5},{4,2},{5,3},{6,0},{7,1},{8,14},{9,15},{10,... | collective-permute-start | bytes 30728 | tf_op jit(solution)/shard_map/ppermute | solution.py:362
  95.9 3.4 %collective-permute-done.19.refs_3_ = f32[1,2560]{1,0:T(1,128)S(1)} collective-permute-done((f32[1,2560]{1,0:T(1,128)S(1)}, f32[1,2560]{1,0:T(1,128)S(1)}, u32[]{:S(2)}, u32[]{:S(2)}) %collective-permute-start.19) | collective-permute-done | bytes 10272 | tf_op jit(solution)/shard_map/ppermute | solution.py:362
  99.3 0.8 shard_map.72
  (53 shorter events, 2.0 us)
Async XLA Ops:
  0.6 1.2 %copy-start.1 = (bf16[256,2048]{1,0:T(8,128)(2,1)S(1)}, bf16[256,2048]{1,0:T(8,128)(2,1)}, u32[]{:S(2)}) copy-start(bf16[256,2048]{1,0:T(8,128)(2,1)} %emb.1) | copy-start | bytes 3145732
  1.9 0.7 copy-start.2
  2.9 11.3 %collective-permute-start = (bf16[264,2048]{1,0:T(8,128)(2,1)S(1)}, bf16[264,2048]{1,0:T(8,128)(2,1)}, u32[]{:S(2)}, u32[]{:S(2)}) collective-permute-start(bf16[264,2048]{1,0:T(8,128)(2,1)S(1)} %get-tuple-element.40.own.refs_1_), channel_id=1, source_target_pairs={{2,4},{3,5},{4,2},{5,3},{0,1},{1,0},{6,7},{7,6},{10,12},{11,13},{1... | collective-permute-start | bytes 3244040 | tf_op jit(solution)/shard_map/ppermute | solution.py:362
  3.5 27.8 %collective-permute-start.1 = (bf16[264,2048]{1,0:T(8,128)(2,1)S(1)}, bf16[264,2048]{1,0:T(8,128)(2,1)}, u32[]{:S(2)}, u32[]{:S(2)}) collective-permute-start(bf16[264,2048]{1,0:T(8,128)(2,1)S(1)} %get-tuple-element.40.own.refs_1_), channel_id=1, source_target_pairs={{0,2},{1,3},{2,0},{3,1},{4,6},{5,7},{6,4},{7,5},{8,10},{9,11},{10,... | collective-permute-start | bytes 3244040 | tf_op jit(solution)/shard_map/ppermute | solution.py:362
  7.6 26.2 %collective-permute-start.4 = (bf16[264,2048]{1,0:T(8,128)(2,1)S(1)}, bf16[264,2048]{1,0:T(8,128)(2,1)}, u32[]{:S(2)}, u32[]{:S(2)}) collective-permute-start(bf16[264,2048]{1,0:T(8,128)(2,1)S(1)} %get-tuple-element.40.own.refs_1_), channel_id=1, source_target_pairs={{0,8},{8,0},{16,24},{24,16},{1,9},{9,1},{17,25},{25,17},{2,10},{10... | collective-permute-start | bytes 3244040 | tf_op jit(solution)/shard_map/ppermute | solution.py:363
  9.1 28.2 %collective-permute-start.7 = (bf16[264,2048]{1,0:T(8,128)(2,1)S(1)}, bf16[264,2048]{1,0:T(8,128)(2,1)}, u32[]{:S(2)}, u32[]{:S(2)}) collective-permute-start(bf16[264,2048]{1,0:T(8,128)(2,1)S(1)} %get-tuple-element.40.own.refs_1_), channel_id=1, source_target_pairs={{0,1},{1,0},{2,3},{3,2},{4,5},{5,4},{6,7},{7,6},{8,9},{9,8},{10,11... | collective-permute-start | bytes 3244040 | tf_op jit(solution)/shard_map/ppermute | solution.py:362
  9.1 26.3 %collective-permute-start.6 = (bf16[264,2048]{1,0:T(8,128)(2,1)S(1)}, bf16[264,2048]{1,0:T(8,128)(2,1)S(1)}, u32[]{:S(2)}, u32[]{:S(2)}) collective-permute-start(bf16[264,2048]{1,0:T(8,128)(2,1)S(1)} %get-tuple-element.40.own.refs_1_), channel_id=1, source_target_pairs={{0,16},{8,24},{16,0},{24,8},{1,17},{9,25},{17,1},{25,9},{2,18},{10... | collective-permute-start | bytes 3244040 | tf_op jit(solution)/shard_map/ppermute | solution.py:363
  12.0 23.4 %copy-start = (bf16[128,2048]{1,0:T(8,128)(2,1)S(1)}, bf16[128,2048]{1,0:T(8,128)(2,1)}, u32[]{:S(2)}) copy-start(bf16[128,2048]{1,0:T(8,128)(2,1)} %refs_11_.1) | copy-start | bytes 1572868
  31.3 13.0 %collective-permute-start.2 = (bf16[264,2048]{1,0:T(8,128)(2,1)}, bf16[264,2048]{1,0:T(8,128)(2,1)S(1)}, u32[]{:S(2)}, u32[]{:S(2)}) collective-permute-start(bf16[264,2048]{1,0:T(8,128)(2,1)} %collective-permute-done.1.x0), channel_id=1, source_target_pairs={{2,4},{3,5},{4,2},{5,3},{0,1},{1,0},{6,7},{7,6},{10,12},{11,13},{1... | collective-permute-start | bytes 3244040 | tf_op jit(solution)/shard_map/ppermute | solution.py:362
  31.3 26.5 %collective-permute-start.3 = (bf16[264,2048]{1,0:T(8,128)(2,1)}, bf16[264,2048]{1,0:T(8,128)(2,1)S(1)}, u32[]{:S(2)}, u32[]{:S(2)}) collective-permute-start(bf16[264,2048]{1,0:T(8,128)(2,1)} %collective-permute-done.m1), channel_id=1, source_target_pairs={{0,2},{1,3},{2,0},{3,1},{4,6},{5,7},{6,4},{7,5},{8,10},{9,11},{10,... | collective-permute-start | bytes 3244040 | tf_op jit(solution)/shard_map/ppermute | solution.py:362
  33.8 5.1 %collective-permute-start.5 = (bf16[264,2048]{1,0:T(8,128)(2,1)}, bf16[264,2048]{1,0:T(8,128)(2,1)S(1)}, u32[]{:S(2)}, u32[]{:S(2)}) collective-permute-start(bf16[264,2048]{1,0:T(8,128)(2,1)} %collective-permute-done.4.gx.refs_3_), channel_id=1, source_target_pairs={{0,1},{1,0},{2,3},{3,2},{4,5},{5,4},{6,7},{7,6},{8,9},{9,8},{10,11... | collective-permute-start | bytes 3244040 | tf_op jit(solution)/shard_map/ppermute | solution.py:362
  35.5 25.6 %collective-permute-start.8 = (bf16[264,2048]{1,0:T(8,128)(2,1)S(1)}, bf16[264,2048]{1,0:T(8,128)(2,1)S(1)}, u32[]{:S(2)}, u32[]{:S(2)}) collective-permute-start(bf16[264,2048]{1,0:T(8,128)(2,1)S(1)} %pad_maximum_fusion), channel_id=1, source_target_pairs={{0,8},{8,0},{16,24},{24,16},{1,9},{9,1},{17,25},{25,17},{2,10},{10... | collective-permute-start | bytes 3244040 | tf_op jit(solution)/shard_map/ppermute | solution.py:363
  37.3 24.8 %collective-permute-start.10 = (bf16[256,2048]{1,0:T(8,128)(2,1)S(1)}, bf16[256,2048]{1,0:T(8,128)(2,1)S(1)}, u32[]{:S(2)}, u32[]{:S(2)}) collective-permute-start(bf16[256,2048]{1,0:T(8,128)(2,1)S(1)} %pad_maximum_fusion.1), channel_id=1, source_target_pairs={{0,16},{8,24},{16,0},{24,8},{1,17},{9,25},{17,1},{25,9},{2,18},{10... | collective-permute-start | bytes 3145736 | tf_op jit(solution)/shard_map/ppermute | solution.py:363
  57.8 9.9 %collective-permute-start.13 = (bf16[264,2048]{1,0:T(8,128)(2,1)S(1)}, bf16[264,2048]{1,0:T(8,128)(2,1)S(1)}, u32[]{:S(2)}, u32[]{:S(2)}) collective-permute-start(bf16[264,2048]{1,0:T(8,128)(2,1)S(1)} %collective-permute-done.6.gy.refs_5_), channel_id=1, source_target_pairs={{0,1},{1,0},{2,3},{3,2},{4,5},{5,4},{6,7},{7,6},{8,9},{9,8},{10,11... | collective-permute-start | bytes 3244040 | tf_op jit(solution)/shard_map/ppermute | solution.py:362
  61.1 6.6 %collective-permute-start.14 = (bf16[264,2048]{1,0:T(8,128)(2,1)S(1)}, bf16[264,2048]{1,0:T(8,128)(2,1)S(1)}, u32[]{:S(2)}, u32[]{:S(2)}) collective-permute-start(bf16[264,2048]{1,0:T(8,128)(2,1)S(1)} %collective-permute-done.8.hx.refs_7_), channel_id=1, source_target_pairs={{0,1},{1,0},{2,3},{3,2},{4,5},{5,4},{6,7},{7,6},{8,9},{9,8},{10,11... | collective-permute-start | bytes 3244040 | tf_op jit(solution)/shard_map/ppermute | solution.py:362
  62.1 3.2 %collective-permute-start.11 = (bf16[256,2048]{1,0:T(8,128)(2,1)S(1)}, bf16[256,2048]{1,0:T(8,128)(2,1)S(1)}, u32[]{:S(2)}, u32[]{:S(2)}) collective-permute-start(bf16[256,2048]{1,0:T(8,128)(2,1)S(1)} %collective-permute-done.10.hy.refs_9_), channel_id=1, source_target_pairs={{0,1},{1,0},{2,3},{3,2},{4,5},{5,4},{6,7},{7,6},{8,9},{9,8},{10,11... | collective-permute-start | bytes 3145736 | tf_op jit(solution)/shard_map/ppermute | solution.py:362
  62.1 4.8 %collective-permute-start.15 = (bf16[128,2048]{1,0:T(8,128)(2,1)S(1)}, bf16[128,2048]{1,0:T(8,128)(2,1)S(1)}, u32[]{:S(2)}, u32[]{:S(2)}) collective-permute-start(bf16[128,2048]{1,0:T(8,128)(2,1)S(1)} %copy-done), channel_id=1, source_target_pairs={{0,1},{1,0},{2,3},{3,2},{4,5},{5,4},{6,7},{7,6},{8,9},{9,8},{10,11... | collective-permute-start | bytes 1572872 | tf_op jit(solution)/shard_map/ppermute | solution.py:362
  62.6 26.1 %collective-permute-start.16 = (bf16[264,2048]{1,0:T(8,128)(2,1)S(1)}, bf16[264,2048]{1,0:T(8,128)(2,1)S(1)}, u32[]{:S(2)}, u32[]{:S(2)}) collective-permute-start(bf16[264,2048]{1,0:T(8,128)(2,1)S(1)} %collective-permute-done.2.m3), channel_id=1, source_target_pairs={{0,2},{1,3},{2,0},{3,1},{4,6},{5,7},{6,4},{7,5},{8,10},{9,11},{10,... | collective-permute-start | bytes 3244040 | tf_op jit(solution)/shard_map/ppermute | solution.py:362
  65.3 14.0 %collective-permute-start.9 = (bf16[128,2048]{1,0:T(8,128)(2,1)S(1)}, bf16[128,2048]{1,0:T(8,128)(2,1)S(1)}, u32[]{:S(2)}, u32[]{:S(2)}) collective-permute-start(bf16[128,2048]{1,0:T(8,128)(2,1)S(1)} %slice.24), channel_id=1, source_target_pairs={{0,16},{8,24},{16,0},{24,8},{1,17},{9,25},{17,1},{25,9},{2,18},{10... | collective-permute-start | bytes 1572872 | tf_op jit(solution)/shard_map/ppermute | solution.py:363
  66.8 13.8 %collective-permute-start.12 = (bf16[128,2048]{1,0:T(8,128)(2,1)S(1)}, bf16[128,2048]{1,0:T(8,128)(2,1)S(1)}, u32[]{:S(2)}, u32[]{:S(2)}) collective-permute-start(bf16[128,2048]{1,0:T(8,128)(2,1)S(1)} %slice.26), channel_id=1, source_target_pairs={{0,8},{8,0},{16,24},{24,16},{1,9},{9,1},{17,25},{25,17},{2,10},{10... | collective-permute-start | bytes 1572872 | tf_op jit(solution)/shard_map/ppermute | solution.py:363
  83.3 10.5 %collective-permute-start.17 = (f32[1,2560]{1,0:T(1,128)S(1)}, f32[1,2560]{1,0:T(1,128)S(1)}, u32[]{:S(2)}, u32[]{:S(2)}) collective-permute-start(f32[1,2560]{1,0:T(1,128)S(1)} %get-tuple-element.67), channel_id=1, source_target_pairs={{0,2},{1,3},{2,0},{3,1},{4,6},{5,7},{6,4},{7,5},{8,10},{9,11},{10,... | collective-permute-start | bytes 30728 | tf_op jit(solution)/shard_map/ppermute | solution.py:362
  83.8 9.9 %collective-permute-start.18 = (f32[1,2560]{1,0:T(1,128)S(1)}, f32[1,2560]{1,0:T(1,128)S(1)}, u32[]{:S(2)}, u32[]{:S(2)}) collective-permute-start(f32[1,2560]{1,0:T(1,128)S(1)} %get-tuple-element.68), channel_id=1, source_target_pairs={{0,4},{1,5},{2,6},{3,7},{4,0},{5,1},{6,2},{7,3},{8,12},{9,13},{10,... | collective-permute-start | bytes 30728 | tf_op jit(solution)/shard_map/ppermute | solution.py:362
  93.8 5.5 %collective-permute-start.19 = (f32[1,2560]{1,0:T(1,128)S(1)}, f32[1,2560]{1,0:T(1,128)S(1)}, u32[]{:S(2)}, u32[]{:S(2)}) collective-permute-start(f32[1,2560]{1,0:T(1,128)S(1)} %shard_map.71), channel_id=1, source_target_pairs={{0,6},{1,7},{2,4},{3,5},{4,2},{5,3},{6,0},{7,1},{8,14},{9,15},{10,... | collective-permute-start | bytes 30728 | tf_op jit(solution)/shard_map/ppermute | solution.py:362

commit v3 on v2

--- a/solution.py
+++ b/solution.py
@@ -117,6 +117,7 @@
 
 
 lowest = -1e30
+ANY = pl.BlockSpec(memory_space=pl.ANY)
 VMEM = pl.BlockSpec(memory_space=pltpu.VMEM)
 SMEM = pl.BlockSpec(memory_space=pltpu.SMEM)
 
@@ -206,19 +207,22 @@
     return ref[pl.ds(0, 256), :], read_note(ref[pl.ds(256, 8), :])[0][0:1]
 
 
-def choose(target, first, second, pos):
-    layer = pos[1] // 2
-    mid = (layer == 1) | (layer == 2)
-
+def fetch(source, target, sem):
+    copy = pltpu.make_async_copy(source, target, sem)
+    copy.start()
+    return copy
+
+
+def fetch_choice(first, second, target, sem, mid):
     @pl.when(mid)
     def _():
-        target[...] = first[...]
+        fetch(first, target, sem)
 
     @pl.when(jnp.logical_not(mid))
     def _():
-        target[...] = second[...]
-
-    return mid
+        fetch(second, target, sem)
+
+    return pltpu.make_async_copy(first, target, sem)
 
 
 def in_the_middle(pos):
@@ -242,19 +246,26 @@
 
 def first_kernel(
     pos, own, own_s, gx, gx_s, gy, gy_s, hx, hx_s, hy, hy_s, cents, cents_s, x0, m1, x1, m3, noise, noise_far, early,
-    early_sums, early_columns, result, sums, columns, near,
+    early_sums, early_columns, result, sums, columns, inner, near, sib, across, sems,
 ):
-    mid = choose(near, m1, x1, pos)
+    mid = in_the_middle(pos)
+    inner_copy = fetch(x0, inner, sems.at[0])
+    near_copy = fetch_choice(m1, x1, near, sems.at[1], mid)
+    others = [fetch(own_s, sib, sems.at[2]), fetch(gx, across, sems.at[3])]
     pieces, notes = blocks_of((gy, gy_s), ((hy, hx), (hy_s, hx_s)))
     write_columns(columns, notes)
-    before = blocks_of((own, own_s, gx, gx_s), ())[0]
+    before = blocks_of((own, sib, across, gx_s), ())[0]
     cent_pieces = [(ref, 0, 128) for ref in (cents, cents_s, hx, hx_s, hy, hy_s)]
-    for number, ref in enumerate((own, x0, near)):
+    for number, (ref, copy) in enumerate(((own, None), (inner, inner_copy), (near, near_copy))):
+        if copy is not None:
+            copy.wait()
         rows, cluster = named_rows(ref)
         sim = similarity(pieces, columns, rows, cluster)
         lanes = slice(256 * number, 256 * number + 256)
         score = top(inverse_temp * product(stack(cent_pieces), rows) + noise[:, lanes])
         result[number] = jnp.concatenate([score, jnp.maximum(sim, early[number])], axis=0)
+    for copy in others:
+        copy.wait()
     sums[...] = early_sums[...] + sums_of(pos, pieces, notes)
 
     @pl.when(mid)
@@ -270,28 +281,21 @@
         result[2] = jnp.concatenate([result[2][0:1], jnp.maximum(result[2][1:2], sim)], axis=0)
 
 
-def whole_visit(rows, cluster, layer_refs, columns, noise):
-    own, own_s, gx, gx_s, gy, gy_s, hx, hx_s, hy, hy_s, cents, cents_s, d, d_s = layer_refs
-    first = blocks_of((own, own_s, gx, gx_s), ())[0]
-    second = blocks_of((gy, gy_s), ((hy, hx), (hy_s, hx_s)))[0]
-    sim = similarity(first, columns[0], rows, cluster)
-    sim = jnp.maximum(sim, similarity(second, columns[1], rows, cluster))
-    pieces = [(ref, 0, 128) for ref in (cents, cents_s, hx, hx_s, hy, hy_s, d, d_s)]
-    return top(inverse_temp * product(stack(pieces), rows) + noise[...]), sim
-
-
 def second_kernel(
-    pos, own, x0, m1, x1, m3, d, d_s, noise, noise_far, before, sums, mine, by_one, by_two, by_three, near,
+    pos, own, x0, m1, x1, m3, d, d_s, noise, noise_far, before, sums, mine, by_one, by_two, by_three, inner, near, sems,
 ):
-    mid = choose(near, m1, x1, pos)
+    mid = in_the_middle(pos)
+    copies = [None, fetch(x0, inner, sems.at[0]), fetch_choice(m1, x1, near, sems.at[1], mid)]
     layer = pos[1] // 2
     cents = stack([(d, 0, 128), (d_s, 0, 128)])
 
     def visit(number, ref, values):
+        if number in (1, 2):
+            copies[number].wait()
         score = top(inverse_temp * product(cents, ref[pl.ds(0, 256), :]) + values)
         return jnp.maximum(score, before[number][0:1]), before[number][1:2]
 
-    results = [visit(i, ref, noise[:, 256 * i : 256 * i + 256]) for i, ref in enumerate((own, x0, near))]
+    results = [visit(i, ref, noise[:, 256 * i : 256 * i + 256]) for i, ref in enumerate((own, inner, near))]
     mine[:, 0:256], mine[:, 256:512] = results[0]
     by_one[:, 0:256], by_one[:, 256:512] = results[1]
     for bits, out in ((0, mine), (1, by_one), (2, by_two), (3, by_three)):
@@ -308,15 +312,25 @@
         by_three[:, 0:512] = jnp.full((1, 512), lowest, jnp.float32)
 
 
-def last_kernel(*refs):
-    pos, layer_refs, (x2, noise_far), columns, (before, out) = refs[0], refs[1:15], refs[15:17], refs[17:19], refs[19:]
-    layer = pos[1] // 2
+def last_kernel(
+    pos, own, own_s, gx, gx_s, gy, gy_s, hx, hx_s, hy, hy_s, cents, cents_s, d, d_s, x2, noise, early_columns, columns,
+    before, out, sib, across, sems,
+):
     out[...] = before[...]
 
-    @pl.when((layer == 0) | (layer == 3))
-    def _():
+    @pl.when(jnp.logical_not(in_the_middle(pos)))
+    def _():
+        others = [fetch(own_s, sib, sems.at[0]), fetch(gx, across, sems.at[1])]
         rows, cluster = named_rows(x2)
-        out[:, 0:256], out[:, 256:512] = whole_visit(rows, cluster, layer_refs, columns, noise_far)
+        pieces = [(ref, 0, 128) for ref in (cents, cents_s, hx, hx_s, hy, hy_s, d, d_s)]
+        score = top(inverse_temp * product(stack(pieces), rows) + noise[...])
+        pieces = blocks_of((gy, gy_s), ((hy, hx), (hy_s, hx_s)))[0]
+        sim = similarity(pieces, columns, rows, cluster)
+        for copy in others:
+            copy.wait()
+        pieces = blocks_of((own, sib, across, gx_s), ())[0]
+        sim = jnp.maximum(sim, similarity(pieces, early_columns, rows, cluster))
+        out[:, 0:256], out[:, 256:512] = score, sim
 
 
 def final_kernel(scale, *refs):
@@ -331,11 +345,11 @@
     center_out[...] = total * lax.rsqrt(jnp.mean(total * total) + epsilon)
 
 
-def call(kernel, inputs, out_shapes, scratch, flops, mib, scalars=1):
+def call(kernel, inputs, out_shapes, scratch, flops, mib, scalars=1, fetched=()):
     return pl.pallas_call(
         kernel,
         out_shape=[jax.ShapeDtypeStruct(shape, dtype) for shape, dtype in out_shapes],
-        in_specs=[SMEM] * scalars + [VMEM] * (len(inputs) - scalars),
+        in_specs=[SMEM if i < scalars else ANY if i in fetched else VMEM for i in range(len(inputs))],
         out_specs=[VMEM] * len(out_shapes),
         scratch_shapes=scratch,
         compiler_params=pltpu.CompilerParams(vmem_limit_bytes=mib * 1024 * 1024),
@@ -413,15 +427,16 @@
     d_s = by(hy_s[:128], by_x)
 
     layer_pieces = [own, own_s, gx, gx_s, gy, gy_s, hx, hx_s, hy, hy_s, centroids, cents_s]
-    one_block = [pltpu.VMEM((noted, feature_dim), bf16)]
+    blocks = lambda count: [pltpu.VMEM((noted, feature_dim), bf16)] * count + [pltpu.SemaphoreType.DMA((count,))]
     message = ((1, 2 * rows_dev + feature_dim), f32)
     result, sums, columns = call(
         first_kernel,
         [pos] + layer_pieces + [x0, m1, x1, m3, noises[0], noises[2]] + early,
         [((4, 2, rows_dev), f32), ((8, feature_dim), f32), ((half, 256), f32)],
-        one_block,
+        blocks(4),
         2 * 256 * 6400 * feature_dim,
         20,
+        fetched=(2, 3, 13, 14, 15),
     )
     d, d_s, result = together((d, d_s, result))
     columns = [early[2], columns]
@@ -429,9 +444,10 @@
         second_kernel,
         [pos, own, x0, m1, x1, m3, d, d_s, noises[1], noises[2], result, sums],
         [message] * 4,
-        one_block,
+        blocks(2),
         1,
         20,
+        fetched=(2, 3, 4),
     )
     one, two = rows(by_one, flip(1)), rows(by_two, flip(2))
     x2, by_three = together((x2, by_three))
@@ -439,9 +455,10 @@
         last_kernel,
         [pos] + layer_pieces + [d, d_s, x2, noises[2]] + columns + [by_three],
         [message],
-        [],
+        blocks(2),
         1,
         20,
+        fetched=(2, 3),
     )
     by_three, one, two = together((by_three, one, two))
     three = rows(by_three, flip(3))

time: 100 us -> 102 us (1.020)
  Pallas kernels: 24.7 us -> 26.8 us
    pallas_call x6, Pallas kernels: 24.7 us -> 26.8 us  [call(): pl.pallas_call(kernel, out_shape=[jax.ShapeDtypeStruct(shape, dtype) for...]
  transfers between devices with their start and end apart: 20 -> 20, of which waited for: 10 -> 10; matrix products, arithmetic and copies ran while one was open for 4% -> 4% of each run, Pallas kernels for 24% -> 25%
where the time goes in v3:
time: 102 us
  waiting for transfers between devices  47.3 us (46%)
  Pallas kernels  26.8 us (26%)
  starting transfers between devices  19.7 us (19%)
  local copies, waits for them, and re-layouts  3.08 us (3%)
  other arithmetic  3.05 us (3%)
  between operations  1.6 us (2%)
    ppermute x14, waiting for transfers between devices, box_shards(): rows = lambda value, pairs: lax.ppermute(value, 'rows', pairs)  39 us
    pallas_call x6, Pallas kernels, call(): pl.pallas_call(kernel, out_shape=[jax.ShapeDtypeStruct(shape, dtype) for...  26.8 us
    ppermute x14, starting transfers between devices, box_shards(): rows = lambda value, pairs: lax.ppermute(value, 'rows', pairs)  12.1 us
    ppermute x6, waiting for transfers between devices, box_shards(): by = lambda value, pairs: lax.ppermute(value, 'cent', pairs)  8.39 us
    ppermute x6, starting transfers between devices, box_shards(): by = lambda value, pairs: lax.ppermute(value, 'cent', pairs)  7.53 us
    neg x3, other arithmetic, gumbel_noise(): return -jnp.log(-jnp.log(uniform))  2.67 us
  transfers between devices with their start and end apart: 20, of which 10 were waited for; matrix products, arithmetic and copies ran while one was open for 4% of the time, Pallas kernels for 25%

profile of v3, /device:TPU:0, one launch (start us, length us, event | category | flops | bytes accessed | tf_op | source)
XLA Modules:
  0.0 101.5 jit_solution(2915697543195557304)
XLA Ops:
  0.6 1.2 %copy-done.1 = bf16[256,2048]{1,0:T(8,128)(2,1)S(1)} copy-done((bf16[256,2048]{1,0:T(8,128)(2,1)S(1)}, bf16[256,2048]{1,0:T(8,128)(2,1)}, u32[]{:S(2)}) %copy-start.1) | copy-done | bytes 1048600
  1.9 0.7 copy-done.2
  3.5 4.1 %collective-permute-start.1 = (bf16[264,2048]{1,0:T(8,128)(2,1)S(1)}, bf16[264,2048]{1,0:T(8,128)(2,1)}, u32[]{:S(2)}, u32[]{:S(2)}) collective-permute-start(bf16[264,2048]{1,0:T(8,128)(2,1)S(1)} %get-tuple-element.40.own), channel_id=1, source_target_pairs={{0,2},{1,3},{2,0},{3,1},{4,6},{5,7},{6,4},{7,5},{8,10},{9,11},{10,... | collective-permute-start | bytes 3244040 | tf_op jit(solution)/shard_map/ppermute | solution.py:376
  7.6 1.5 %collective-permute-start.4 = (bf16[264,2048]{1,0:T(8,128)(2,1)S(1)}, bf16[264,2048]{1,0:T(8,128)(2,1)}, u32[]{:S(2)}, u32[]{:S(2)}) collective-permute-start(bf16[264,2048]{1,0:T(8,128)(2,1)S(1)} %get-tuple-element.40.own), channel_id=1, source_target_pairs={{0,8},{8,0},{16,24},{24,16},{1,9},{9,1},{17,25},{25,17},{2,10},{10... | collective-permute-start | bytes 3244040 | tf_op jit(solution)/shard_map/ppermute | solution.py:377
  9.1 1.5 %collective-permute-start.6 = (bf16[264,2048]{1,0:T(8,128)(2,1)S(1)}, bf16[264,2048]{1,0:T(8,128)(2,1)S(1)}, u32[]{:S(2)}, u32[]{:S(2)}) collective-permute-start(bf16[264,2048]{1,0:T(8,128)(2,1)S(1)} %get-tuple-element.40.own), channel_id=1, source_target_pairs={{0,16},{8,24},{16,0},{24,8},{1,17},{9,25},{17,1},{25,9},{2,18},{10... | collective-permute-start | bytes 3244040 | tf_op jit(solution)/shard_map/ppermute | solution.py:377
  11.5 0.5 fusion.29.noise
  12.1 0.7 fusion.19.noise_far.noise
  12.8 1.4 %fusion.9.noise = f32[768,768]{1,0:T(8,128)S(1)} fusion(s32[]{:T(128)} %bitcast.6, s32[768]{0:T(1024)S(1)} %broadcast_multiply_fusion.1, s32[768]{0:T(1024)S(1)} %add_multiply_fusion), kind=kLoop, calls=%fused_computation.12 | loop fusion | flops 9437184 | bytes 2365444 | tf_op jit(solution)/shard_map/neg | solution.py:27
  14.3 17.0 %collective-permute-done.1.x0 = bf16[264,2048]{1,0:T(8,128)(2,1)} collective-permute-done((bf16[264,2048]{1,0:T(8,128)(2,1)S(1)}, bf16[264,2048]{1,0:T(8,128)(2,1)}, u32[]{:S(2)}, u32[]{:S(2)}) %collective-permute-start.1) | collective-permute-done | bytes 1081376 | tf_op jit(solution)/shard_map/ppermute | solution.py:376
  31.3 2.5 %collective-permute-start.3 = (bf16[264,2048]{1,0:T(8,128)(2,1)}, bf16[264,2048]{1,0:T(8,128)(2,1)S(1)}, u32[]{:S(2)}, u32[]{:S(2)}) collective-permute-start(bf16[264,2048]{1,0:T(8,128)(2,1)} %collective-permute-done.m1), channel_id=1, source_target_pairs={{0,2},{1,3},{2,0},{3,1},{4,6},{5,7},{6,4},{7,5},{8,10},{9,11},{10,... | collective-permute-start | bytes 3244040 | tf_op jit(solution)/shard_map/ppermute | solution.py:376
  33.8 1.5 %collective-permute-done.6.gy = bf16[264,2048]{1,0:T(8,128)(2,1)S(1)} collective-permute-done((bf16[264,2048]{1,0:T(8,128)(2,1)S(1)}, bf16[264,2048]{1,0:T(8,128)(2,1)S(1)}, u32[]{:S(2)}, u32[]{:S(2)}) %collective-permute-start.6) | collective-permute-done | bytes 1081376 | tf_op jit(solution)/shard_map/ppermute | solution.py:377
  35.5 0.6 collective-permute-start.8
  36.1 1.1 %slice.25 = bf16[128,2048]{1,0:T(8,128)(2,1)S(1)} slice(bf16[264,2048]{1,0:T(8,128)(2,1)} %collective-permute-done.4.gx), slice={[0:128], [0:2048]} | slice | bytes 1048576 | tf_op jit(solution)/shard_map/slice | solution.py:412
  37.3 1.6 %collective-permute-start.10 = (bf16[256,2048]{1,0:T(8,128)(2,1)S(1)}, bf16[256,2048]{1,0:T(8,128)(2,1)S(1)}, u32[]{:S(2)}, u32[]{:S(2)}) collective-permute-start(bf16[256,2048]{1,0:T(8,128)(2,1)S(1)} %pad_maximum_fusion.1), channel_id=1, source_target_pairs={{0,16},{8,24},{16,0},{24,8},{1,17},{9,25},{17,1},{25,9},{2,18},{10... | collective-permute-start | bytes 3145736 | tf_op jit(solution)/shard_map/ppermute | solution.py:377
  39.0 5.3 %shard_map.68 = (f32[3,1,256]{2,1,0:T(1,128)S(1)}, f32[8,2048]{1,0:T(8,128)S(1)}, f32[1024,256]{1,0:T(8,128)S(1)}) custom-call(s32[2]{0:T(128)S(1)} %pad_add_fusion.pos, bf16[264,2048]{1,0:T(8,128)(2,1)S(1)} %get-tuple-element.40.own, bf16[264,2048]{1,0:T(8,128)(2,1)} %collective-permute-done.7.own_s, bf16[264,2048]{1,0:T(8,128)(2,1)} %collective-permute-done.4.gx, ...), custom_call_target="tpu_custom_call" | custom-call | flops 2147483648 | bytes 8388608 | tf_op jit(solution)/shard_map/pallas_call | solution.py:349
  44.3 13.5 %collective-permute-done.3.x1 = bf16[264,2048]{1,0:T(8,128)(2,1)S(1)} collective-permute-done((bf16[264,2048]{1,0:T(8,128)(2,1)}, bf16[264,2048]{1,0:T(8,128)(2,1)S(1)}, u32[]{:S(2)}, u32[]{:S(2)}) %collective-permute-start.3) | collective-permute-done | bytes 1081376 | tf_op jit(solution)/shard_map/ppermute | solution.py:376
  57.8 3.3 %collective-permute-done.8.hx = bf16[264,2048]{1,0:T(8,128)(2,1)S(1)} collective-permute-done((bf16[264,2048]{1,0:T(8,128)(2,1)S(1)}, bf16[264,2048]{1,0:T(8,128)(2,1)S(1)}, u32[]{:S(2)}, u32[]{:S(2)}) %collective-permute-start.8) | collective-permute-done | bytes 1081376 | tf_op jit(solution)/shard_map/ppermute | solution.py:377
  61.1 1.0 collective-permute-done.10.hy
  62.6 2.7 %collective-permute-done.11.hy_s = bf16[256,2048]{1,0:T(8,128)(2,1)S(1)} collective-permute-done((bf16[256,2048]{1,0:T(8,128)(2,1)S(1)}, bf16[256,2048]{1,0:T(8,128)(2,1)S(1)}, u32[]{:S(2)}, u32[]{:S(2)}) %collective-permute-start.11) | collective-permute-done | bytes 1048608 | tf_op jit(solution)/shard_map/ppermute | solution.py:376
  65.3 1.5 %collective-permute-start.9 = (bf16[128,2048]{1,0:T(8,128)(2,1)S(1)}, bf16[128,2048]{1,0:T(8,128)(2,1)S(1)}, u32[]{:S(2)}, u32[]{:S(2)}) collective-permute-start(bf16[128,2048]{1,0:T(8,128)(2,1)S(1)} %slice.24), channel_id=1, source_target_pairs={{0,16},{8,24},{16,0},{24,8},{1,17},{9,25},{17,1},{25,9},{2,18},{10... | collective-permute-start | bytes 1572872 | tf_op jit(solution)/shard_map/ppermute | solution.py:377
  66.8 0.8 collective-permute-start.12
  67.7 10.4 %shard_map.69 = (f32[4,2,256]{2,1,0:T(2,128)S(1)}, f32[8,2048]{1,0:T(8,128)S(1)}, f32[1024,256]{1,0:T(8,128)S(1)}) custom-call(s32[2]{0:T(128)S(1)} %pad_add_fusion.pos, bf16[264,2048]{1,0:T(8,128)(2,1)S(1)} %get-tuple-element.40.own, bf16[264,2048]{1,0:T(8,128)(2,1)} %collective-permute-done.7.own_s, bf16[264,2048]{1,0:T(8,128)(2,1)} %collective-permute-done.4.gx, ...), custom_call_target="tpu_custom_call" | custom-call | flops 6710886400 | bytes 8388608 | tf_op jit(solution)/shard_map/pallas_call | solution.py:349
  78.1 1.2 %collective-permute-done.9.d = bf16[128,2048]{1,0:T(8,128)(2,1)S(1)} collective-permute-done((bf16[128,2048]{1,0:T(8,128)(2,1)S(1)}, bf16[128,2048]{1,0:T(8,128)(2,1)S(1)}, u32[]{:S(2)}, u32[]{:S(2)}) %collective-permute-start.9) | collective-permute-done | bytes 524320 | tf_op jit(solution)/shard_map/ppermute | solution.py:377
  79.2 1.4 %collective-permute-done.12.d_s = bf16[128,2048]{1,0:T(8,128)(2,1)S(1)} collective-permute-done((bf16[128,2048]{1,0:T(8,128)(2,1)S(1)}, bf16[128,2048]{1,0:T(8,128)(2,1)S(1)}, u32[]{:S(2)}, u32[]{:S(2)}) %collective-permute-start.12) | collective-permute-done | bytes 524320 | tf_op jit(solution)/shard_map/ppermute | solution.py:377
  80.6 3.3 %shard_map.70 = (f32[1,2560]{1,0:T(1,128)S(1)}, f32[1,2560]{1,0:T(1,128)S(1)}, f32[1,2560]{1,0:T(1,128)S(1)}, f32[1,2560]{1,0:T(1,128)S(1)}) custom-call(s32[2]{0:T(128)S(1)} %pad_add_fusion.pos, bf16[264,2048]{1,0:T(8,128)(2,1)S(1)} %get-tuple-element.40.own, bf16[264,2048]{1,0:T(8,128)(2,1)} %collective-permute-done.1.x0, ...), custom_call_target="tpu_custom_call" | custom-call | flops 1 | bytes 8388608 | tf_op jit(solution)/shard_map/pallas_call | solution.py:349
  83.9 0.5 collective-permute-start.17
  84.4 1.7 %collective-permute-start.18 = (f32[1,2560]{1,0:T(1,128)S(1)}, f32[1,2560]{1,0:T(1,128)S(1)}, u32[]{:S(2)}, u32[]{:S(2)}) collective-permute-start(f32[1,2560]{1,0:T(1,128)S(1)} %get-tuple-element.68), channel_id=1, source_target_pairs={{0,4},{1,5},{2,6},{3,7},{4,0},{5,1},{6,2},{7,3},{8,12},{9,13},{10,... | collective-permute-start | bytes 30728 | tf_op jit(solution)/shard_map/ppermute | solution.py:376
  86.1 2.5 %collective-permute-done.16.x2 = bf16[264,2048]{1,0:T(8,128)(2,1)S(1)} collective-permute-done((bf16[264,2048]{1,0:T(8,128)(2,1)S(1)}, bf16[264,2048]{1,0:T(8,128)(2,1)S(1)}, u32[]{:S(2)}, u32[]{:S(2)}) %collective-permute-start.16) | collective-permute-done | bytes 1081376 | tf_op jit(solution)/shard_map/ppermute | solution.py:376
  88.6 6.6 %shard_map.71 = f32[1,2560]{1,0:T(1,128)S(1)} custom-call(s32[2]{0:T(128)S(1)} %pad_add_fusion.pos, bf16[264,2048]{1,0:T(8,128)(2,1)S(1)} %get-tuple-element.40.own, bf16[264,2048]{1,0:T(8,128)(2,1)} %collective-permute-done.7.own_s, bf16[264,2048]{1,0:T(8,128)(2,1)} %collective-permute-done.4.gx, bf16[264,2048]{1,0:T(8,128)(2,1)S(1)} %collective-permute-done.5.gx_s, ...), custom_call_target="tpu_custom_call" | custom-call | flops 1 | bytes 8388608 | tf_op jit(solution)/shard_map/pallas_call | solution.py:349
  95.2 2.2 %collective-permute-start.19 = (f32[1,2560]{1,0:T(1,128)S(1)}, f32[1,2560]{1,0:T(1,128)S(1)}, u32[]{:S(2)}, u32[]{:S(2)}) collective-permute-start(f32[1,2560]{1,0:T(1,128)S(1)} %shard_map.71), channel_id=1, source_target_pairs={{0,6},{1,7},{2,4},{3,5},{4,2},{5,3},{6,0},{7,1},{8,14},{9,15},{10,... | collective-permute-start | bytes 30728 | tf_op jit(solution)/shard_map/ppermute | solution.py:376
  97.4 3.3 %collective-permute-done.19.refs_3_ = f32[1,2560]{1,0:T(1,128)S(1)} collective-permute-done((f32[1,2560]{1,0:T(1,128)S(1)}, f32[1,2560]{1,0:T(1,128)S(1)}, u32[]{:S(2)}, u32[]{:S(2)}) %collective-permute-start.19) | collective-permute-done | bytes 10272 | tf_op jit(solution)/shard_map/ppermute | solution.py:376
  100.7 0.8 shard_map.72
  (53 shorter events, 2.0 us)
Async XLA Ops:
  0.6 1.2 %copy-start.1 = (bf16[256,2048]{1,0:T(8,128)(2,1)S(1)}, bf16[256,2048]{1,0:T(8,128)(2,1)}, u32[]{:S(2)}) copy-start(bf16[256,2048]{1,0:T(8,128)(2,1)} %emb.1) | copy-start | bytes 3145732
  1.9 0.7 copy-start.2
  2.9 11.3 %collective-permute-start = (bf16[264,2048]{1,0:T(8,128)(2,1)S(1)}, bf16[264,2048]{1,0:T(8,128)(2,1)}, u32[]{:S(2)}, u32[]{:S(2)}) collective-permute-start(bf16[264,2048]{1,0:T(8,128)(2,1)S(1)} %get-tuple-element.40.own), channel_id=1, source_target_pairs={{2,4},{3,5},{4,2},{5,3},{0,1},{1,0},{6,7},{7,6},{10,12},{11,13},{1... | collective-permute-start | bytes 3244040 | tf_op jit(solution)/shard_map/ppermute | solution.py:376
  3.5 27.8 %collective-permute-start.1 = (bf16[264,2048]{1,0:T(8,128)(2,1)S(1)}, bf16[264,2048]{1,0:T(8,128)(2,1)}, u32[]{:S(2)}, u32[]{:S(2)}) collective-permute-start(bf16[264,2048]{1,0:T(8,128)(2,1)S(1)} %get-tuple-element.40.own), channel_id=1, source_target_pairs={{0,2},{1,3},{2,0},{3,1},{4,6},{5,7},{6,4},{7,5},{8,10},{9,11},{10,... | collective-permute-start | bytes 3244040 | tf_op jit(solution)/shard_map/ppermute | solution.py:376
  7.6 26.2 %collective-permute-start.4 = (bf16[264,2048]{1,0:T(8,128)(2,1)S(1)}, bf16[264,2048]{1,0:T(8,128)(2,1)}, u32[]{:S(2)}, u32[]{:S(2)}) collective-permute-start(bf16[264,2048]{1,0:T(8,128)(2,1)S(1)} %get-tuple-element.40.own), channel_id=1, source_target_pairs={{0,8},{8,0},{16,24},{24,16},{1,9},{9,1},{17,25},{25,17},{2,10},{10... | collective-permute-start | bytes 3244040 | tf_op jit(solution)/shard_map/ppermute | solution.py:377
  9.1 28.2 %collective-permute-start.7 = (bf16[264,2048]{1,0:T(8,128)(2,1)S(1)}, bf16[264,2048]{1,0:T(8,128)(2,1)}, u32[]{:S(2)}, u32[]{:S(2)}) collective-permute-start(bf16[264,2048]{1,0:T(8,128)(2,1)S(1)} %get-tuple-element.40.own), channel_id=1, source_target_pairs={{0,1},{1,0},{2,3},{3,2},{4,5},{5,4},{6,7},{7,6},{8,9},{9,8},{10,11... | collective-permute-start | bytes 3244040 | tf_op jit(solution)/shard_map/ppermute | solution.py:376
  9.1 26.3 %collective-permute-start.6 = (bf16[264,2048]{1,0:T(8,128)(2,1)S(1)}, bf16[264,2048]{1,0:T(8,128)(2,1)S(1)}, u32[]{:S(2)}, u32[]{:S(2)}) collective-permute-start(bf16[264,2048]{1,0:T(8,128)(2,1)S(1)} %get-tuple-element.40.own), channel_id=1, source_target_pairs={{0,16},{8,24},{16,0},{24,8},{1,17},{9,25},{17,1},{25,9},{2,18},{10... | collective-permute-start | bytes 3244040 | tf_op jit(solution)/shard_map/ppermute | solution.py:377
  12.0 23.4 %copy-start = (bf16[128,2048]{1,0:T(8,128)(2,1)S(1)}, bf16[128,2048]{1,0:T(8,128)(2,1)}, u32[]{:S(2)}) copy-start(bf16[128,2048]{1,0:T(8,128)(2,1)} %cents.3) | copy-start | bytes 1572868
  31.3 13.0 %collective-permute-start.2 = (bf16[264,2048]{1,0:T(8,128)(2,1)}, bf16[264,2048]{1,0:T(8,128)(2,1)S(1)}, u32[]{:S(2)}, u32[]{:S(2)}) collective-permute-start(bf16[264,2048]{1,0:T(8,128)(2,1)} %collective-permute-done.1.x0), channel_id=1, source_target_pairs={{2,4},{3,5},{4,2},{5,3},{0,1},{1,0},{6,7},{7,6},{10,12},{11,13},{1... | collective-permute-start | bytes 3244040 | tf_op jit(solution)/shard_map/ppermute | solution.py:376
  31.3 26.5 %collective-permute-start.3 = (bf16[264,2048]{1,0:T(8,128)(2,1)}, bf16[264,2048]{1,0:T(8,128)(2,1)S(1)}, u32[]{:S(2)}, u32[]{:S(2)}) collective-permute-start(bf16[264,2048]{1,0:T(8,128)(2,1)} %collective-permute-done.m1), channel_id=1, source_target_pairs={{0,2},{1,3},{2,0},{3,1},{4,6},{5,7},{6,4},{7,5},{8,10},{9,11},{10,... | collective-permute-start | bytes 3244040 | tf_op jit(solution)/shard_map/ppermute | solution.py:376
  33.8 5.1 %collective-permute-start.5 = (bf16[264,2048]{1,0:T(8,128)(2,1)}, bf16[264,2048]{1,0:T(8,128)(2,1)S(1)}, u32[]{:S(2)}, u32[]{:S(2)}) collective-permute-start(bf16[264,2048]{1,0:T(8,128)(2,1)} %collective-permute-done.4.gx), channel_id=1, source_target_pairs={{0,1},{1,0},{2,3},{3,2},{4,5},{5,4},{6,7},{7,6},{8,9},{9,8},{10,11... | collective-permute-start | bytes 3244040 | tf_op jit(solution)/shard_map/ppermute | solution.py:376
  35.5 25.6 %collective-permute-start.8 = (bf16[264,2048]{1,0:T(8,128)(2,1)S(1)}, bf16[264,2048]{1,0:T(8,128)(2,1)S(1)}, u32[]{:S(2)}, u32[]{:S(2)}) collective-permute-start(bf16[264,2048]{1,0:T(8,128)(2,1)S(1)} %pad_maximum_fusion), channel_id=1, source_target_pairs={{0,8},{8,0},{16,24},{24,16},{1,9},{9,1},{17,25},{25,17},{2,10},{10... | collective-permute-start | bytes 3244040 | tf_op jit(solution)/shard_map/ppermute | solution.py:377
  37.3 24.8 %collective-permute-start.10 = (bf16[256,2048]{1,0:T(8,128)(2,1)S(1)}, bf16[256,2048]{1,0:T(8,128)(2,1)S(1)}, u32[]{:S(2)}, u32[]{:S(2)}) collective-permute-start(bf16[256,2048]{1,0:T(8,128)(2,1)S(1)} %pad_maximum_fusion.1), channel_id=1, source_target_pairs={{0,16},{8,24},{16,0},{24,8},{1,17},{9,25},{17,1},{25,9},{2,18},{10... | collective-permute-start | bytes 3145736 | tf_op jit(solution)/shard_map/ppermute | solution.py:377
  57.8 9.9 %collective-permute-start.13 = (bf16[264,2048]{1,0:T(8,128)(2,1)S(1)}, bf16[264,2048]{1,0:T(8,128)(2,1)S(1)}, u32[]{:S(2)}, u32[]{:S(2)}) collective-permute-start(bf16[264,2048]{1,0:T(8,128)(2,1)S(1)} %collective-permute-done.6.gy), channel_id=1, source_target_pairs={{0,1},{1,0},{2,3},{3,2},{4,5},{5,4},{6,7},{7,6},{8,9},{9,8},{10,11... | collective-permute-start | bytes 3244040 | tf_op jit(solution)/shard_map/ppermute | solution.py:376
  61.1 6.6 %collective-permute-start.14 = (bf16[264,2048]{1,0:T(8,128)(2,1)S(1)}, bf16[264,2048]{1,0:T(8,128)(2,1)S(1)}, u32[]{:S(2)}, u32[]{:S(2)}) collective-permute-start(bf16[264,2048]{1,0:T(8,128)(2,1)S(1)} %collective-permute-done.8.hx), channel_id=1, source_target_pairs={{0,1},{1,0},{2,3},{3,2},{4,5},{5,4},{6,7},{7,6},{8,9},{9,8},{10,11... | collective-permute-start | bytes 3244040 | tf_op jit(solution)/shard_map/ppermute | solution.py:376
  62.1 3.2 %collective-permute-start.11 = (bf16[256,2048]{1,0:T(8,128)(2,1)S(1)}, bf16[256,2048]{1,0:T(8,128)(2,1)S(1)}, u32[]{:S(2)}, u32[]{:S(2)}) collective-permute-start(bf16[256,2048]{1,0:T(8,128)(2,1)S(1)} %collective-permute-done.10.hy), channel_id=1, source_target_pairs={{0,1},{1,0},{2,3},{3,2},{4,5},{5,4},{6,7},{7,6},{8,9},{9,8},{10,11... | collective-permute-start | bytes 3145736 | tf_op jit(solution)/shard_map/ppermute | solution.py:376
  62.1 4.8 %collective-permute-start.15 = (bf16[128,2048]{1,0:T(8,128)(2,1)S(1)}, bf16[128,2048]{1,0:T(8,128)(2,1)S(1)}, u32[]{:S(2)}, u32[]{:S(2)}) collective-permute-start(bf16[128,2048]{1,0:T(8,128)(2,1)S(1)} %copy-done), channel_id=1, source_target_pairs={{0,1},{1,0},{2,3},{3,2},{4,5},{5,4},{6,7},{7,6},{8,9},{9,8},{10,11... | collective-permute-start | bytes 1572872 | tf_op jit(solution)/shard_map/ppermute | solution.py:376
  62.6 26.0 %collective-permute-start.16 = (bf16[264,2048]{1,0:T(8,128)(2,1)S(1)}, bf16[264,2048]{1,0:T(8,128)(2,1)S(1)}, u32[]{:S(2)}, u32[]{:S(2)}) collective-permute-start(bf16[264,2048]{1,0:T(8,128)(2,1)S(1)} %collective-permute-done.2.m3), channel_id=1, source_target_pairs={{0,2},{1,3},{2,0},{3,1},{4,6},{5,7},{6,4},{7,5},{8,10},{9,11},{10,... | collective-permute-start | bytes 3244040 | tf_op jit(solution)/shard_map/ppermute | solution.py:376
  65.3 14.0 %collective-permute-start.9 = (bf16[128,2048]{1,0:T(8,128)(2,1)S(1)}, bf16[128,2048]{1,0:T(8,128)(2,1)S(1)}, u32[]{:S(2)}, u32[]{:S(2)}) collective-permute-start(bf16[128,2048]{1,0:T(8,128)(2,1)S(1)} %slice.24), channel_id=1, source_target_pairs={{0,16},{8,24},{16,0},{24,8},{1,17},{9,25},{17,1},{25,9},{2,18},{10... | collective-permute-start | bytes 1572872 | tf_op jit(solution)/shard_map/ppermute | solution.py:377
  66.8 13.8 %collective-permute-start.12 = (bf16[128,2048]{1,0:T(8,128)(2,1)S(1)}, bf16[128,2048]{1,0:T(8,128)(2,1)S(1)}, u32[]{:S(2)}, u32[]{:S(2)}) collective-permute-start(bf16[128,2048]{1,0:T(8,128)(2,1)S(1)} %slice.26), channel_id=1, source_target_pairs={{0,8},{8,0},{16,24},{24,16},{1,9},{9,1},{17,25},{25,17},{2,10},{10... | collective-permute-start | bytes 1572872 | tf_op jit(solution)/shard_map/ppermute | solution.py:377
  83.9 11.3 %collective-permute-start.17 = (f32[1,2560]{1,0:T(1,128)S(1)}, f32[1,2560]{1,0:T(1,128)S(1)}, u32[]{:S(2)}, u32[]{:S(2)}) collective-permute-start(f32[1,2560]{1,0:T(1,128)S(1)} %get-tuple-element.67), channel_id=1, source_target_pairs={{0,2},{1,3},{2,0},{3,1},{4,6},{5,7},{6,4},{7,5},{8,10},{9,11},{10,... | collective-permute-start | bytes 30728 | tf_op jit(solution)/shard_map/ppermute | solution.py:376
  84.4 10.8 %collective-permute-start.18 = (f32[1,2560]{1,0:T(1,128)S(1)}, f32[1,2560]{1,0:T(1,128)S(1)}, u32[]{:S(2)}, u32[]{:S(2)}) collective-permute-start(f32[1,2560]{1,0:T(1,128)S(1)} %get-tuple-element.68), channel_id=1, source_target_pairs={{0,4},{1,5},{2,6},{3,7},{4,0},{5,1},{6,2},{7,3},{8,12},{9,13},{10,... | collective-permute-start | bytes 30728 | tf_op jit(solution)/shard_map/ppermute | solution.py:376
  95.2 5.5 %collective-permute-start.19 = (f32[1,2560]{1,0:T(1,128)S(1)}, f32[1,2560]{1,0:T(1,128)S(1)}, u32[]{:S(2)}, u32[]{:S(2)}) collective-permute-start(f32[1,2560]{1,0:T(1,128)S(1)} %shard_map.71), channel_id=1, source_target_pairs={{0,6},{1,7},{2,4},{3,5},{4,2},{5,3},{6,0},{7,1},{8,14},{9,15},{10,... | collective-permute-start | bytes 30728 | tf_op jit(solution)/shard_map/ppermute | solution.py:376

commit v4 on v2

--- a/solution.py
+++ b/solution.py
@@ -117,6 +117,7 @@
 
 
 lowest = -1e30
+HEAD = 32
 VMEM = pl.BlockSpec(memory_space=pltpu.VMEM)
 SMEM = pl.BlockSpec(memory_space=pltpu.SMEM)
 
@@ -270,16 +271,6 @@
         result[2] = jnp.concatenate([result[2][0:1], jnp.maximum(result[2][1:2], sim)], axis=0)
 
 
-def whole_visit(rows, cluster, layer_refs, columns, noise):
-    own, own_s, gx, gx_s, gy, gy_s, hx, hx_s, hy, hy_s, cents, cents_s, d, d_s = layer_refs
-    first = blocks_of((own, own_s, gx, gx_s), ())[0]
-    second = blocks_of((gy, gy_s), ((hy, hx), (hy_s, hx_s)))[0]
-    sim = similarity(first, columns[0], rows, cluster)
-    sim = jnp.maximum(sim, similarity(second, columns[1], rows, cluster))
-    pieces = [(ref, 0, 128) for ref in (cents, cents_s, hx, hx_s, hy, hy_s, d, d_s)]
-    return top(inverse_temp * product(stack(pieces), rows) + noise[...]), sim
-
-
 def second_kernel(
     pos, own, x0, m1, x1, m3, d, d_s, noise, noise_far, before, sums, mine, by_one, by_two, by_three, near,
 ):
@@ -308,15 +299,22 @@
         by_three[:, 0:512] = jnp.full((1, 512), lowest, jnp.float32)
 
 
-def last_kernel(*refs):
-    pos, layer_refs, (x2, noise_far), columns, (before, out) = refs[0], refs[1:15], refs[15:17], refs[17:19], refs[19:]
-    layer = pos[1] // 2
+def last_kernel(
+    pos, own, own_s, gx, gx_s, gy, gy_s, hx, hx_s, hy, hy_s, cents, cents_s, d, d_s, head, tail, noise, early_columns,
+    columns, before, out,
+):
     out[...] = before[...]
 
-    @pl.when((layer == 0) | (layer == 3))
-    def _():
-        rows, cluster = named_rows(x2)
-        out[:, 0:256], out[:, 256:512] = whole_visit(rows, cluster, layer_refs, columns, noise_far)
+    @pl.when(jnp.logical_not(in_the_middle(pos)))
+    def _():
+        rows = jnp.concatenate([head[...], tail[pl.ds(0, 256 - HEAD), :]], axis=0)
+        cluster = read_note(tail[pl.ds(256 - HEAD, 8), :])[0][0:1]
+        first = blocks_of((own, own_s, gx, gx_s), ())[0]
+        second = blocks_of((gy, gy_s), ((hy, hx), (hy_s, hx_s)))[0]
+        sim = similarity(first, early_columns, rows, cluster)
+        out[:, 256:512] = jnp.maximum(sim, similarity(second, columns, rows, cluster))
+        pieces = [(ref, 0, 128) for ref in (cents, cents_s, hx, hx_s, hy, hy_s, d, d_s)]
+        out[:, 0:256] = top(inverse_temp * product(stack(pieces), rows) + noise[...])
 
 
 def final_kernel(scale, *refs):
@@ -357,6 +355,7 @@
 
     sibling = [(i, i ^ 1) for i in range(8)]
     across = along([(1, 2), (2, 1)]) + sibling[0:2] + sibling[6:8]
+    between_ends = along([(0, 3), (3, 0)]) + sibling[2:6]
     flip = lambda bits: along([(z, z ^ bits) for z in range(4)])
     by_x, by_y = [(i, i ^ 1) for i in range(4)], [(i, i ^ 2) for i in range(4)]
     rows = lambda value, pairs: lax.ppermute(value, "rows", pairs)
@@ -391,8 +390,9 @@
         noise(visitors[:768], layer_cents[768:]),
         noise(visitors[768:], layer_cents),
     ]
-    m1, x0, *noises = together((m1, x0, *noises))
+    m1, x0, head, *noises = together((m1, x0, own[:HEAD], *noises))
     m3, x1 = rows(x0, across), rows(m1, flip(1))
+    far_head = rows(head, between_ends)
 
     hx = by(jnp.concatenate([centroids, gy[128:]], axis=0), by_x)
     hy = by(jnp.concatenate([centroids, gx[:128]], axis=0), by_y)
@@ -406,9 +406,9 @@
         2 * 512 * 1024 * feature_dim,
         16,
     )
-    m3, x1, gx_s, gy, cents, *early = together((m3, x1, gx_s, gy, centroids, *early))
-
-    x2, d = rows(m3, flip(1)), by(hx[:128], by_y)
+    m3, x1, far_head, far_tail, gx_s, gy, cents, *early = together((m3, x1, far_head, own[HEAD:], gx_s, gy, centroids, *early))
+
+    far_tail, d = rows(far_tail, between_ends), by(hx[:128], by_y)
     gy_s, hx_s, hy_s, cents_s = rows(gy, sibling), rows(hx, sibling), rows(hy, sibling), rows(cents, sibling)
     d_s = by(hy_s[:128], by_x)
 
@@ -434,10 +434,10 @@
         20,
     )
     one, two = rows(by_one, flip(1)), rows(by_two, flip(2))
-    x2, by_three = together((x2, by_three))
+    far_tail, by_three = together((far_tail, by_three))
     (by_three,) = call(
         last_kernel,
-        [pos] + layer_pieces + [d, d_s, x2, noises[2]] + columns + [by_three],
+        [pos] + layer_pieces + [d, d_s, far_head, far_tail, noises[2]] + columns + [by_three],
         [message],
         [],
         1,

time: 100 us -> 99.8 us (level)
  waiting for transfers between devices: 48.1 us -> 42.7 us
  starting transfers between devices: 19.5 us -> 24.3 us
    ppermute x6, waiting for transfers between devices: 8.3 us -> 3.27 us  [box_shards(): by = lambda value, pairs: lax.ppermute(value, 'cent', pairs)]
    ppermute x14 -> x15, starting transfers between devices: 12 us -> 16 us  [box_shards(): rows = lambda value, pairs: lax.ppermute(value, 'rows', pairs)]
    ppermute x14 -> x15, waiting for transfers between devices: 39.8 us -> 39.4 us  [box_shards(): rows = lambda value, pairs: lax.ppermute(value, 'rows', pairs)]
  transfers between devices with their start and end apart: 20 -> 21, of which waited for: 10 -> 7; matrix products, arithmetic and copies ran while one was open for 4% -> 4% of each run, Pallas kernels for 24% -> 24%
where the time goes in v4:
time: 99.8 us; the launch traced here: 99.5 us
  waiting for transfers between devices  42.7 us (43%)
  Pallas kernels  24.7 us (25%)
  starting transfers between devices  24.3 us (24%)
  local copies, waits for them, and re-layouts  3.16 us (3%)
  other arithmetic  3.04 us (3%)
  between operations  1.64 us (2%)
    ppermute x15, waiting for transfers between devices, box_shards(): rows = lambda value, pairs: lax.ppermute(value, 'rows', pairs)  39.4 us
    pallas_call x6, Pallas kernels, call(): pl.pallas_call(kernel, out_shape=[jax.ShapeDtypeStruct(shape, dtype) for...  24.7 us
    ppermute x15, starting transfers between devices, box_shards(): rows = lambda value, pairs: lax.ppermute(value, 'rows', pairs)  16 us
    ppermute x6, starting transfers between devices, box_shards(): by = lambda value, pairs: lax.ppermute(value, 'cent', pairs)  8.27 us
    ppermute x6, waiting for transfers between devices, box_shards(): by = lambda value, pairs: lax.ppermute(value, 'cent', pairs)  3.27 us
    neg x3, other arithmetic, gumbel_noise(): return -jnp.log(-jnp.log(uniform))  2.67 us
  transfers between devices with their start and end apart: 21, of which 7 were waited for; matrix products, arithmetic and copies ran while one was open for 4% of the time, Pallas kernels for 24%

profile of v4, /device:TPU:0, one launch (start us, length us, event | category | flops | bytes accessed | tf_op | source)
XLA Modules:
  0.0 99.5 jit_solution(10681654439185437039)
XLA Ops:
  0.6 1.2 %copy-done.1 = bf16[256,2048]{1,0:T(8,128)(2,1)S(1)} copy-done((bf16[256,2048]{1,0:T(8,128)(2,1)S(1)}, bf16[256,2048]{1,0:T(8,128)(2,1)}, u32[]{:S(2)}) %copy-start.1) | copy-done | bytes 1048600
  1.9 0.7 copy-done.2
  2.9 0.5 collective-permute-start
  3.5 4.1 %collective-permute-start.1 = (bf16[264,2048]{1,0:T(8,128)(2,1)S(1)}, bf16[264,2048]{1,0:T(8,128)(2,1)}, u32[]{:S(2)}, u32[]{:S(2)}) collective-permute-start(bf16[264,2048]{1,0:T(8,128)(2,1)S(1)} %get-tuple-element.43.own), channel_id=1, source_target_pairs={{0,2},{1,3},{2,0},{3,1},{4,6},{5,7},{6,4},{7,5},{8,10},{9,11},{10,... | collective-permute-start | bytes 3244040 | tf_op jit(solution)/shard_map/ppermute | solution.py:361
  7.6 1.5 %collective-permute-start.5 = (bf16[264,2048]{1,0:T(8,128)(2,1)S(1)}, bf16[264,2048]{1,0:T(8,128)(2,1)}, u32[]{:S(2)}, u32[]{:S(2)}) collective-permute-start(bf16[264,2048]{1,0:T(8,128)(2,1)S(1)} %get-tuple-element.43.own), channel_id=1, source_target_pairs={{0,8},{8,0},{16,24},{24,16},{1,9},{9,1},{17,25},{25,17},{2,10},{10... | collective-permute-start | bytes 3244040 | tf_op jit(solution)/shard_map/ppermute | solution.py:362
  9.1 1.5 %collective-permute-start.7 = (bf16[264,2048]{1,0:T(8,128)(2,1)S(1)}, bf16[264,2048]{1,0:T(8,128)(2,1)S(1)}, u32[]{:S(2)}, u32[]{:S(2)}) collective-permute-start(bf16[264,2048]{1,0:T(8,128)(2,1)S(1)} %get-tuple-element.43.own), channel_id=1, source_target_pairs={{0,16},{8,24},{16,0},{24,8},{1,17},{9,25},{17,1},{25,9},{2,18},{10... | collective-permute-start | bytes 3244040 | tf_op jit(solution)/shard_map/ppermute | solution.py:362
  11.5 0.5 fusion.29.noise
  12.1 0.7 fusion.19.noise_far.noise
  12.8 1.4 %fusion.9.noise = f32[768,768]{1,0:T(8,128)S(1)} fusion(s32[]{:T(128)} %bitcast.6, s32[768]{0:T(1024)S(1)} %broadcast_multiply_fusion.1, s32[768]{0:T(1024)S(1)} %add_multiply_fusion), kind=kLoop, calls=%fused_computation.12 | loop fusion | flops 9437184 | bytes 2365444 | tf_op jit(solution)/shard_map/neg | solution.py:27
  14.3 17.0 %collective-permute-done.1.x0 = bf16[264,2048]{1,0:T(8,128)(2,1)} collective-permute-done((bf16[264,2048]{1,0:T(8,128)(2,1)S(1)}, bf16[264,2048]{1,0:T(8,128)(2,1)}, u32[]{:S(2)}, u32[]{:S(2)}) %collective-permute-start.1) | collective-permute-done | bytes 1081376 | tf_op jit(solution)/shard_map/ppermute | solution.py:361
  31.3 2.5 %collective-permute-start.3 = (bf16[264,2048]{1,0:T(8,128)(2,1)}, bf16[264,2048]{1,0:T(8,128)(2,1)S(1)}, u32[]{:S(2)}, u32[]{:S(2)}) collective-permute-start(bf16[264,2048]{1,0:T(8,128)(2,1)} %collective-permute-done.m1), channel_id=1, source_target_pairs={{0,2},{1,3},{2,0},{3,1},{4,6},{5,7},{6,4},{7,5},{8,10},{9,11},{10,... | collective-permute-start | bytes 3244040 | tf_op jit(solution)/shard_map/ppermute | solution.py:361
  33.8 1.5 %collective-permute-done.7.gy = bf16[264,2048]{1,0:T(8,128)(2,1)S(1)} collective-permute-done((bf16[264,2048]{1,0:T(8,128)(2,1)S(1)}, bf16[264,2048]{1,0:T(8,128)(2,1)S(1)}, u32[]{:S(2)}, u32[]{:S(2)}) %collective-permute-start.7) | collective-permute-done | bytes 1081376 | tf_op jit(solution)/shard_map/ppermute | solution.py:362
  35.5 0.6 collective-permute-start.9
  36.1 1.1 %slice.33 = bf16[128,2048]{1,0:T(8,128)(2,1)S(1)} slice(bf16[264,2048]{1,0:T(8,128)(2,1)} %collective-permute-done.5.gx), slice={[0:128], [0:2048]} | slice | bytes 1048576 | tf_op jit(solution)/shard_map/slice | solution.py:398
  37.3 1.6 %collective-permute-start.11 = (bf16[256,2048]{1,0:T(8,128)(2,1)S(1)}, bf16[256,2048]{1,0:T(8,128)(2,1)S(1)}, u32[]{:S(2)}, u32[]{:S(2)}) collective-permute-start(bf16[256,2048]{1,0:T(8,128)(2,1)S(1)} %pad_maximum_fusion.1), channel_id=1, source_target_pairs={{0,16},{8,24},{16,0},{24,8},{1,17},{9,25},{17,1},{25,9},{2,18},{10... | collective-permute-start | bytes 3145736 | tf_op jit(solution)/shard_map/ppermute | solution.py:362
  39.0 1.6 %collective-permute-start.4 = (bf16[32,2048]{1,0:T(8,128)(2,1)S(1)}, bf16[32,2048]{1,0:T(8,128)(2,1)S(1)}, u32[]{:S(2)}, u32[]{:S(2)}) collective-permute-start(bf16[32,2048]{1,0:T(8,128)(2,1)S(1)} %slice.25), channel_id=1, source_target_pairs={{0,6},{1,7},{6,0},{7,1},{2,3},{3,2},{4,5},{5,4},{8,14},{9,15},{14,... | collective-permute-start | bytes 393224 | tf_op jit(solution)/shard_map/ppermute | solution.py:361
  40.6 5.3 %shard_map.68 = (f32[3,1,256]{2,1,0:T(1,128)S(1)}, f32[8,2048]{1,0:T(8,128)S(1)}, f32[1024,256]{1,0:T(8,128)S(1)}) custom-call(s32[2]{0:T(128)S(1)} %pad_add_fusion.pos, bf16[264,2048]{1,0:T(8,128)(2,1)S(1)} %get-tuple-element.43.own, bf16[264,2048]{1,0:T(8,128)(2,1)} %collective-permute-done.8.own_s, bf16[264,2048]{1,0:T(8,128)(2,1)} %collective-permute-done.5.gx, ...), custom_call_target="tpu_custom_call" | custom-call | flops 2147483648 | bytes 8388608 | tf_op jit(solution)/shard_map/pallas_call | solution.py:333
  45.9 16.1 %collective-permute-done.4.head = bf16[32,2048]{1,0:T(8,128)(2,1)S(1)} collective-permute-done((bf16[32,2048]{1,0:T(8,128)(2,1)S(1)}, bf16[32,2048]{1,0:T(8,128)(2,1)S(1)}, u32[]{:S(2)}, u32[]{:S(2)}) %collective-permute-start.4) | collective-permute-done | bytes 131104 | tf_op jit(solution)/shard_map/ppermute | solution.py:361
  62.0 0.5 collective-permute-start.15
  62.6 0.4 collective-permute-start.16
  63.0 1.7 %collective-permute-start.17 = (bf16[232,2048]{1,0:T(8,128)(2,1)S(1)}, bf16[232,2048]{1,0:T(8,128)(2,1)S(1)}, u32[]{:S(2)}, u32[]{:S(2)}) collective-permute-start(bf16[232,2048]{1,0:T(8,128)(2,1)S(1)} %slice.26), channel_id=1, source_target_pairs={{0,6},{1,7},{6,0},{7,1},{2,3},{3,2},{4,5},{5,4},{8,14},{9,15},{14,... | collective-permute-start | bytes 2850824 | tf_op jit(solution)/shard_map/ppermute | solution.py:361
  64.8 3.0 %collective-permute-done.12.hy_s = bf16[256,2048]{1,0:T(8,128)(2,1)S(1)} collective-permute-done((bf16[256,2048]{1,0:T(8,128)(2,1)S(1)}, bf16[256,2048]{1,0:T(8,128)(2,1)S(1)}, u32[]{:S(2)}, u32[]{:S(2)}) %collective-permute-start.12) | collective-permute-done | bytes 1048608 | tf_op jit(solution)/shard_map/ppermute | solution.py:361
  67.8 1.5 %collective-permute-start.10 = (bf16[128,2048]{1,0:T(8,128)(2,1)S(1)}, bf16[128,2048]{1,0:T(8,128)(2,1)S(1)}, u32[]{:S(2)}, u32[]{:S(2)}) collective-permute-start(bf16[128,2048]{1,0:T(8,128)(2,1)S(1)} %slice.32), channel_id=1, source_target_pairs={{0,16},{8,24},{16,0},{24,8},{1,17},{9,25},{17,1},{25,9},{2,18},{10... | collective-permute-start | bytes 1572872 | tf_op jit(solution)/shard_map/ppermute | solution.py:362
  69.3 1.6 %collective-permute-start.13 = (bf16[128,2048]{1,0:T(8,128)(2,1)S(1)}, bf16[128,2048]{1,0:T(8,128)(2,1)S(1)}, u32[]{:S(2)}, u32[]{:S(2)}) collective-permute-start(bf16[128,2048]{1,0:T(8,128)(2,1)S(1)} %slice.34), channel_id=1, source_target_pairs={{0,8},{8,0},{16,24},{24,16},{1,9},{9,1},{17,25},{25,17},{2,10},{10... | collective-permute-start | bytes 1572872 | tf_op jit(solution)/shard_map/ppermute | solution.py:362
  70.9 10.5 %shard_map.69 = (f32[4,2,256]{2,1,0:T(2,128)S(1)}, f32[8,2048]{1,0:T(8,128)S(1)}, f32[1024,256]{1,0:T(8,128)S(1)}) custom-call(s32[2]{0:T(128)S(1)} %pad_add_fusion.pos, bf16[264,2048]{1,0:T(8,128)(2,1)S(1)} %get-tuple-element.43.own, bf16[264,2048]{1,0:T(8,128)(2,1)} %collective-permute-done.8.own_s, bf16[264,2048]{1,0:T(8,128)(2,1)} %collective-permute-done.5.gx, ...), custom_call_target="tpu_custom_call" | custom-call | flops 6710886400 | bytes 8388608 | tf_op jit(solution)/shard_map/pallas_call | solution.py:333
  81.7 1.4 %collective-permute-done.13.d_s = bf16[128,2048]{1,0:T(8,128)(2,1)S(1)} collective-permute-done((bf16[128,2048]{1,0:T(8,128)(2,1)S(1)}, bf16[128,2048]{1,0:T(8,128)(2,1)S(1)}, u32[]{:S(2)}, u32[]{:S(2)}) %collective-permute-start.13) | collective-permute-done | bytes 524320 | tf_op jit(solution)/shard_map/ppermute | solution.py:362
  83.1 2.7 %shard_map.70 = (f32[1,2560]{1,0:T(1,128)S(1)}, f32[1,2560]{1,0:T(1,128)S(1)}, f32[1,2560]{1,0:T(1,128)S(1)}, f32[1,2560]{1,0:T(1,128)S(1)}) custom-call(s32[2]{0:T(128)S(1)} %pad_add_fusion.pos, bf16[264,2048]{1,0:T(8,128)(2,1)S(1)} %get-tuple-element.43.own, bf16[264,2048]{1,0:T(8,128)(2,1)} %collective-permute-done.1.x0, ...), custom_call_target="tpu_custom_call" | custom-call | flops 1 | bytes 8388608 | tf_op jit(solution)/shard_map/pallas_call | solution.py:333
  85.8 2.3 %collective-permute-start.19 = (f32[1,2560]{1,0:T(1,128)S(1)}, f32[1,2560]{1,0:T(1,128)S(1)}, u32[]{:S(2)}, u32[]{:S(2)}) collective-permute-start(f32[1,2560]{1,0:T(1,128)S(1)} %get-tuple-element.74), channel_id=1, source_target_pairs={{0,4},{1,5},{2,6},{3,7},{4,0},{5,1},{6,2},{7,3},{8,12},{9,13},{10,... | collective-permute-start | bytes 30728 | tf_op jit(solution)/shard_map/ppermute | solution.py:361
  88.1 5.1 %shard_map.71 = f32[1,2560]{1,0:T(1,128)S(1)} custom-call(s32[2]{0:T(128)S(1)} %pad_add_fusion.pos, bf16[264,2048]{1,0:T(8,128)(2,1)S(1)} %get-tuple-element.43.own, bf16[264,2048]{1,0:T(8,128)(2,1)} %collective-permute-done.8.own_s, bf16[264,2048]{1,0:T(8,128)(2,1)} %collective-permute-done.5.gx, bf16[264,2048]{1,0:T(8,128)(2,1)S(1)} %collective-permute-done.6.gx_s, ...), custom_call_target="tpu_custom_call" | custom-call | flops 1 | bytes 8388608 | tf_op jit(solution)/shard_map/pallas_call | solution.py:333
  93.2 2.2 %collective-permute-start.20 = (f32[1,2560]{1,0:T(1,128)S(1)}, f32[1,2560]{1,0:T(1,128)S(1)}, u32[]{:S(2)}, u32[]{:S(2)}) collective-permute-start(f32[1,2560]{1,0:T(1,128)S(1)} %shard_map.71), channel_id=1, source_target_pairs={{0,6},{1,7},{2,4},{3,5},{4,2},{5,3},{6,0},{7,1},{8,14},{9,15},{10,... | collective-permute-start | bytes 30728 | tf_op jit(solution)/shard_map/ppermute | solution.py:361
  95.4 3.4 %collective-permute-done.20.refs_3_ = f32[1,2560]{1,0:T(1,128)S(1)} collective-permute-done((f32[1,2560]{1,0:T(1,128)S(1)}, f32[1,2560]{1,0:T(1,128)S(1)}, u32[]{:S(2)}, u32[]{:S(2)}) %collective-permute-start.20) | collective-permute-done | bytes 10272 | tf_op jit(solution)/shard_map/ppermute | solution.py:361
  98.8 0.8 shard_map.72
  (57 shorter events, 1.5 us)
Async XLA Ops:
  0.6 1.2 %copy-start.1 = (bf16[256,2048]{1,0:T(8,128)(2,1)S(1)}, bf16[256,2048]{1,0:T(8,128)(2,1)}, u32[]{:S(2)}) copy-start(bf16[256,2048]{1,0:T(8,128)(2,1)} %emb.1) | copy-start | bytes 3145732
  1.9 0.7 copy-start.2
  2.9 11.3 %collective-permute-start = (bf16[264,2048]{1,0:T(8,128)(2,1)S(1)}, bf16[264,2048]{1,0:T(8,128)(2,1)}, u32[]{:S(2)}, u32[]{:S(2)}) collective-permute-start(bf16[264,2048]{1,0:T(8,128)(2,1)S(1)} %get-tuple-element.43.own), channel_id=1, source_target_pairs={{2,4},{3,5},{4,2},{5,3},{0,1},{1,0},{6,7},{7,6},{10,12},{11,13},{1... | collective-permute-start | bytes 3244040 | tf_op jit(solution)/shard_map/ppermute | solution.py:361
  3.5 27.8 %collective-permute-start.1 = (bf16[264,2048]{1,0:T(8,128)(2,1)S(1)}, bf16[264,2048]{1,0:T(8,128)(2,1)}, u32[]{:S(2)}, u32[]{:S(2)}) collective-permute-start(bf16[264,2048]{1,0:T(8,128)(2,1)S(1)} %get-tuple-element.43.own), channel_id=1, source_target_pairs={{0,2},{1,3},{2,0},{3,1},{4,6},{5,7},{6,4},{7,5},{8,10},{9,11},{10,... | collective-permute-start | bytes 3244040 | tf_op jit(solution)/shard_map/ppermute | solution.py:361
  7.6 26.2 %collective-permute-start.5 = (bf16[264,2048]{1,0:T(8,128)(2,1)S(1)}, bf16[264,2048]{1,0:T(8,128)(2,1)}, u32[]{:S(2)}, u32[]{:S(2)}) collective-permute-start(bf16[264,2048]{1,0:T(8,128)(2,1)S(1)} %get-tuple-element.43.own), channel_id=1, source_target_pairs={{0,8},{8,0},{16,24},{24,16},{1,9},{9,1},{17,25},{25,17},{2,10},{10... | collective-permute-start | bytes 3244040 | tf_op jit(solution)/shard_map/ppermute | solution.py:362
  9.1 28.2 %collective-permute-start.8 = (bf16[264,2048]{1,0:T(8,128)(2,1)S(1)}, bf16[264,2048]{1,0:T(8,128)(2,1)}, u32[]{:S(2)}, u32[]{:S(2)}) collective-permute-start(bf16[264,2048]{1,0:T(8,128)(2,1)S(1)} %get-tuple-element.43.own), channel_id=1, source_target_pairs={{0,1},{1,0},{2,3},{3,2},{4,5},{5,4},{6,7},{7,6},{8,9},{9,8},{10,11... | collective-permute-start | bytes 3244040 | tf_op jit(solution)/shard_map/ppermute | solution.py:361
  9.1 26.3 %collective-permute-start.7 = (bf16[264,2048]{1,0:T(8,128)(2,1)S(1)}, bf16[264,2048]{1,0:T(8,128)(2,1)S(1)}, u32[]{:S(2)}, u32[]{:S(2)}) collective-permute-start(bf16[264,2048]{1,0:T(8,128)(2,1)S(1)} %get-tuple-element.43.own), channel_id=1, source_target_pairs={{0,16},{8,24},{16,0},{24,8},{1,17},{9,25},{17,1},{25,9},{2,18},{10... | collective-permute-start | bytes 3244040 | tf_op jit(solution)/shard_map/ppermute | solution.py:362
  12.1 23.3 %copy-start = (bf16[128,2048]{1,0:T(8,128)(2,1)S(1)}, bf16[128,2048]{1,0:T(8,128)(2,1)}, u32[]{:S(2)}) copy-start(bf16[128,2048]{1,0:T(8,128)(2,1)} %cents.3) | copy-start | bytes 1572868
  31.3 30.7 %collective-permute-start.2 = (bf16[264,2048]{1,0:T(8,128)(2,1)}, bf16[264,2048]{1,0:T(8,128)(2,1)S(1)}, u32[]{:S(2)}, u32[]{:S(2)}) collective-permute-start(bf16[264,2048]{1,0:T(8,128)(2,1)} %collective-permute-done.1.x0), channel_id=1, source_target_pairs={{2,4},{3,5},{4,2},{5,3},{0,1},{1,0},{6,7},{7,6},{10,12},{11,13},{1... | collective-permute-start | bytes 3244040 | tf_op jit(solution)/shard_map/ppermute | solution.py:361
  31.3 30.7 %collective-permute-start.3 = (bf16[264,2048]{1,0:T(8,128)(2,1)}, bf16[264,2048]{1,0:T(8,128)(2,1)S(1)}, u32[]{:S(2)}, u32[]{:S(2)}) collective-permute-start(bf16[264,2048]{1,0:T(8,128)(2,1)} %collective-permute-done.m1), channel_id=1, source_target_pairs={{0,2},{1,3},{2,0},{3,1},{4,6},{5,7},{6,4},{7,5},{8,10},{9,11},{10,... | collective-permute-start | bytes 3244040 | tf_op jit(solution)/shard_map/ppermute | solution.py:361
  33.8 5.2 %collective-permute-start.6 = (bf16[264,2048]{1,0:T(8,128)(2,1)}, bf16[264,2048]{1,0:T(8,128)(2,1)S(1)}, u32[]{:S(2)}, u32[]{:S(2)}) collective-permute-start(bf16[264,2048]{1,0:T(8,128)(2,1)} %collective-permute-done.5.gx), channel_id=1, source_target_pairs={{0,1},{1,0},{2,3},{3,2},{4,5},{5,4},{6,7},{7,6},{8,9},{9,8},{10,11... | collective-permute-start | bytes 3244040 | tf_op jit(solution)/shard_map/ppermute | solution.py:361
  35.5 26.5 %collective-permute-start.9 = (bf16[264,2048]{1,0:T(8,128)(2,1)S(1)}, bf16[264,2048]{1,0:T(8,128)(2,1)S(1)}, u32[]{:S(2)}, u32[]{:S(2)}) collective-permute-start(bf16[264,2048]{1,0:T(8,128)(2,1)S(1)} %pad_maximum_fusion), channel_id=1, source_target_pairs={{0,8},{8,0},{16,24},{24,16},{1,9},{9,1},{17,25},{25,17},{2,10},{10... | collective-permute-start | bytes 3244040 | tf_op jit(solution)/shard_map/ppermute | solution.py:362
  37.3 25.2 %collective-permute-start.11 = (bf16[256,2048]{1,0:T(8,128)(2,1)S(1)}, bf16[256,2048]{1,0:T(8,128)(2,1)S(1)}, u32[]{:S(2)}, u32[]{:S(2)}) collective-permute-start(bf16[256,2048]{1,0:T(8,128)(2,1)S(1)} %pad_maximum_fusion.1), channel_id=1, source_target_pairs={{0,16},{8,24},{16,0},{24,8},{1,17},{9,25},{17,1},{25,9},{2,18},{10... | collective-permute-start | bytes 3145736 | tf_op jit(solution)/shard_map/ppermute | solution.py:362
  39.0 23.0 %collective-permute-start.4 = (bf16[32,2048]{1,0:T(8,128)(2,1)S(1)}, bf16[32,2048]{1,0:T(8,128)(2,1)S(1)}, u32[]{:S(2)}, u32[]{:S(2)}) collective-permute-start(bf16[32,2048]{1,0:T(8,128)(2,1)S(1)} %slice.25), channel_id=1, source_target_pairs={{0,6},{1,7},{6,0},{7,1},{2,3},{3,2},{4,5},{5,4},{8,14},{9,15},{14,... | collective-permute-start | bytes 393224 | tf_op jit(solution)/shard_map/ppermute | solution.py:361
  62.0 8.9 %collective-permute-start.14 = (bf16[264,2048]{1,0:T(8,128)(2,1)S(1)}, bf16[264,2048]{1,0:T(8,128)(2,1)S(1)}, u32[]{:S(2)}, u32[]{:S(2)}) collective-permute-start(bf16[264,2048]{1,0:T(8,128)(2,1)S(1)} %collective-permute-done.7.gy), channel_id=1, source_target_pairs={{0,1},{1,0},{2,3},{3,2},{4,5},{5,4},{6,7},{7,6},{8,9},{9,8},{10,11... | collective-permute-start | bytes 3244040 | tf_op jit(solution)/shard_map/ppermute | solution.py:361
  62.0 8.9 %collective-permute-start.15 = (bf16[264,2048]{1,0:T(8,128)(2,1)S(1)}, bf16[264,2048]{1,0:T(8,128)(2,1)S(1)}, u32[]{:S(2)}, u32[]{:S(2)}) collective-permute-start(bf16[264,2048]{1,0:T(8,128)(2,1)S(1)} %collective-permute-done.9.hx), channel_id=1, source_target_pairs={{0,1},{1,0},{2,3},{3,2},{4,5},{5,4},{6,7},{7,6},{8,9},{9,8},{10,11... | collective-permute-start | bytes 3244040 | tf_op jit(solution)/shard_map/ppermute | solution.py:361
  62.5 5.2 %collective-permute-start.12 = (bf16[256,2048]{1,0:T(8,128)(2,1)S(1)}, bf16[256,2048]{1,0:T(8,128)(2,1)S(1)}, u32[]{:S(2)}, u32[]{:S(2)}) collective-permute-start(bf16[256,2048]{1,0:T(8,128)(2,1)S(1)} %collective-permute-done.11.hy), channel_id=1, source_target_pairs={{0,1},{1,0},{2,3},{3,2},{4,5},{5,4},{6,7},{7,6},{8,9},{9,8},{10,11... | collective-permute-start | bytes 3145736 | tf_op jit(solution)/shard_map/ppermute | solution.py:361
  62.6 6.7 %collective-permute-start.16 = (bf16[128,2048]{1,0:T(8,128)(2,1)S(1)}, bf16[128,2048]{1,0:T(8,128)(2,1)S(1)}, u32[]{:S(2)}, u32[]{:S(2)}) collective-permute-start(bf16[128,2048]{1,0:T(8,128)(2,1)S(1)} %copy-done), channel_id=1, source_target_pairs={{0,1},{1,0},{2,3},{3,2},{4,5},{5,4},{6,7},{7,6},{8,9},{9,8},{10,11... | collective-permute-start | bytes 1572872 | tf_op jit(solution)/shard_map/ppermute | solution.py:361
  63.0 25.1 %collective-permute-start.17 = (bf16[232,2048]{1,0:T(8,128)(2,1)S(1)}, bf16[232,2048]{1,0:T(8,128)(2,1)S(1)}, u32[]{:S(2)}, u32[]{:S(2)}) collective-permute-start(bf16[232,2048]{1,0:T(8,128)(2,1)S(1)} %slice.26), channel_id=1, source_target_pairs={{0,6},{1,7},{6,0},{7,1},{2,3},{3,2},{4,5},{5,4},{8,14},{9,15},{14,... | collective-permute-start | bytes 2850824 | tf_op jit(solution)/shard_map/ppermute | solution.py:361
  67.8 14.0 %collective-permute-start.10 = (bf16[128,2048]{1,0:T(8,128)(2,1)S(1)}, bf16[128,2048]{1,0:T(8,128)(2,1)S(1)}, u32[]{:S(2)}, u32[]{:S(2)}) collective-permute-start(bf16[128,2048]{1,0:T(8,128)(2,1)S(1)} %slice.32), channel_id=1, source_target_pairs={{0,16},{8,24},{16,0},{24,8},{1,17},{9,25},{17,1},{25,9},{2,18},{10... | collective-permute-start | bytes 1572872 | tf_op jit(solution)/shard_map/ppermute | solution.py:362
  69.3 13.8 %collective-permute-start.13 = (bf16[128,2048]{1,0:T(8,128)(2,1)S(1)}, bf16[128,2048]{1,0:T(8,128)(2,1)S(1)}, u32[]{:S(2)}, u32[]{:S(2)}) collective-permute-start(bf16[128,2048]{1,0:T(8,128)(2,1)S(1)} %slice.34), channel_id=1, source_target_pairs={{0,8},{8,0},{16,24},{24,16},{1,9},{9,1},{17,25},{25,17},{2,10},{10... | collective-permute-start | bytes 1572872 | tf_op jit(solution)/shard_map/ppermute | solution.py:362
  85.8 7.4 %collective-permute-start.18 = (f32[1,2560]{1,0:T(1,128)S(1)}, f32[1,2560]{1,0:T(1,128)S(1)}, u32[]{:S(2)}, u32[]{:S(2)}) collective-permute-start(f32[1,2560]{1,0:T(1,128)S(1)} %get-tuple-element.73), channel_id=1, source_target_pairs={{0,2},{1,3},{2,0},{3,1},{4,6},{5,7},{6,4},{7,5},{8,10},{9,11},{10,... | collective-permute-start | bytes 30728 | tf_op jit(solution)/shard_map/ppermute | solution.py:361
  85.8 7.4 %collective-permute-start.19 = (f32[1,2560]{1,0:T(1,128)S(1)}, f32[1,2560]{1,0:T(1,128)S(1)}, u32[]{:S(2)}, u32[]{:S(2)}) collective-permute-start(f32[1,2560]{1,0:T(1,128)S(1)} %get-tuple-element.74), channel_id=1, source_target_pairs={{0,4},{1,5},{2,6},{3,7},{4,0},{5,1},{6,2},{7,3},{8,12},{9,13},{10,... | collective-permute-start | bytes 30728 | tf_op jit(solution)/shard_map/ppermute | solution.py:361
  93.2 5.5 %collective-permute-start.20 = (f32[1,2560]{1,0:T(1,128)S(1)}, f32[1,2560]{1,0:T(1,128)S(1)}, u32[]{:S(2)}, u32[]{:S(2)}) collective-permute-start(f32[1,2560]{1,0:T(1,128)S(1)} %shard_map.71), channel_id=1, source_target_pairs={{0,6},{1,7},{2,4},{3,5},{4,2},{5,3},{6,0},{7,1},{8,14},{9,15},{10,... | collective-permute-start | bytes 30728 | tf_op jit(solution)/shard_map/ppermute | solution.py:361
